TPU v7x, 32 devices: a whole 2x2x4 slice. The times are simulated.
32 devices in a mesh: dp: 8 (over y, x, core), mp: 4 (over z).
Axes of the slice: x: 2, y: 2, z: 4, core: 2. Of those that a mesh axis runs over, the one named last changes fastest.
Arguments:
- tokens: bfloat16 [8192, 1024], P(('dp', 'mp')), may hold values from -6 to 6
- cotangent: bfloat16 [8192, 1024], P(('dp', 'mp')), may hold values from -6 to 6
- weight_in: float32 [1024, 4096], P('dp', 'mp'), may hold values from -0.1875 to 0.1875
- weight_out: float32 [4096, 1024], P('mp', 'dp'), may hold values from -0.09375 to 0.09375
- moment_in: float32 [1024, 4096], P('dp', 'mp'), may hold values from -4 to 4
- second_in: float32 [1024, 4096], P('dp', 'mp'), may hold values from 0.01 to 1
- moment_out: float32 [4096, 1024], P('mp', 'dp'), may hold values from -4 to 4
- second_out: float32 [4096, 1024], P('mp', 'dp'), may hold values from 0.01 to 1
Outputs:
- input_grad: bfloat16 [8192, 1024], P(('dp', 'mp'))
- new_weight_in: float32 [1024, 4096], P('dp', 'mp')
- new_moment_in: float32 [1024, 4096], P('dp', 'mp')
- new_second_in: float32 [1024, 4096], P('dp', 'mp')
- new_weight_out: float32 [4096, 1024], P('mp', 'dp')
- new_moment_out: float32 [4096, 1024], P('mp', 'dp')
- new_second_out: float32 [4096, 1024], P('mp', 'dp')
All inputs are finite; a program needn't handle non-finite values.
Results may differ from a plain program's by a relative error of at most 0.0071.
Values may be sent and summed in bfloat16 or wider, within the bound.
A program may use at most 64 MiB of HBM per device.

v0:
```python
import jax
import jax.numpy as jnp
from jax import lax
from jax.sharding import PartitionSpec as P

TOK_DEV = 256
STEP = 1000


BETA_ONE = 0.9
BETA_TWO = 0.999
EPSILON = 1e-08
LEARN_RATE = 0.001
DECAY_RATE = 0.1


def normalize(rows):
    values = rows.astype(jnp.float32)
    inverse = lax.rsqrt(jnp.mean(values * values, axis=-1, keepdims=True) + 1e-06)
    return (values * inverse, inverse)


def activate(values):
    return jax.nn.gelu(values, approximate=True)


def adam_step(weight, moment, second, gradient):
    moment_new = BETA_ONE * moment + (1.0 - BETA_ONE) * gradient
    second_new = BETA_TWO * second + (1.0 - BETA_TWO) * gradient * gradient
    first_fix = 1.0 - BETA_ONE ** float(STEP)
    second_fix = 1.0 - BETA_TWO ** float(STEP)
    update = moment_new / first_fix / (jnp.sqrt(second_new / second_fix) + EPSILON)
    weight_new = weight - LEARN_RATE * (update + DECAY_RATE * weight)
    return (weight_new, moment_new, second_new)


def contract_rows(left, right):
    return lax.dot_general(
        left, right, (((0,), (0,)), ((), ())), preferred_element_type=jnp.float32
    )


def shards(tokens, cotangent, weight_in, weight_out, moment_in, second_in, moment_out, second_out):
    normed_f, inverse = normalize(tokens)
    normed_local = normed_f.astype(jnp.bfloat16)
    pieces = (weight_in.astype(jnp.bfloat16), weight_out.astype(jnp.bfloat16))
    weight_in_b, weight_out_b = (
        lax.all_gather(pieces[0], "dp", axis=0, tiled=True),
        lax.all_gather(pieces[1], "dp", axis=1, tiled=True),
    )
    normed = lax.all_gather(normed_local, "mp", axis=0, tiled=True)
    preact = jnp.dot(normed, weight_in_b, preferred_element_type=jnp.float32)
    activated, backward = jax.vjp(activate, preact)
    hidden = activated.astype(jnp.bfloat16)
    upstream = lax.all_gather(cotangent, "mp", axis=0, tiled=True)
    out_partial = contract_rows(hidden, upstream)
    d_hidden = lax.dot_general(
        upstream, weight_out_b, (((1,), (1,)), ((), ())), preferred_element_type=jnp.float32
    )
    d_preact = backward(d_hidden)[0].astype(jnp.bfloat16)
    in_partial = contract_rows(normed, d_preact)
    in_summed, out_summed = (
        lax.psum_scatter(
            in_partial.astype(jnp.bfloat16), "dp", scatter_dimension=0, tiled=True
        ).astype(jnp.float32),
        lax.psum_scatter(
            out_partial.astype(jnp.bfloat16), "dp", scatter_dimension=1, tiled=True
        ).astype(jnp.float32),
    )
    d_normed = lax.psum_scatter(
        lax.dot_general(
            d_preact, weight_in_b, (((1,), (1,)), ((), ())), preferred_element_type=jnp.float32
        ),
        "mp",
        scatter_dimension=0,
        tiled=True,
    )
    d_rows = inverse * (d_normed - normed_f * jnp.mean(d_normed * normed_f, axis=-1, keepdims=True))
    input_grad = d_rows.astype(jnp.bfloat16)
    token_count = TOK_DEV * lax.axis_size("dp") * lax.axis_size("mp")
    grad_scale = 1.0 / jnp.sqrt(jnp.float32(token_count))
    new_weight_in, new_moment_in, new_second_in = adam_step(
        weight_in, moment_in, second_in, in_summed * grad_scale
    )
    new_weight_out, new_moment_out, new_second_out = adam_step(
        weight_out, moment_out, second_out, out_summed * grad_scale
    )
    return (
        input_grad,
        new_weight_in,
        new_moment_in,
        new_second_in,
        new_weight_out,
        new_moment_out,
        new_second_out,
    )


def solution(mesh):
    return jax.shard_map(
        shards,
        mesh=mesh,
        in_specs=(
            P(("dp", "mp"), None),
            P(("dp", "mp"), None),
            P("dp", "mp"),
            P("mp", "dp"),
            P("dp", "mp"),
            P("dp", "mp"),
            P("mp", "dp"),
            P("mp", "dp"),
        ),
        out_specs=(
            P(("dp", "mp"), None),
            P("dp", "mp"),
            P("dp", "mp"),
            P("dp", "mp"),
            P("mp", "dp"),
            P("mp", "dp"),
            P("mp", "dp"),
        ),
        check_vma=False,
    )
```

profile of v0, /device:TPU:0, one launch (start us, length us, event | category | flops | bytes accessed | tf_op | source)
XLA Modules:
  0.0 361.2 jit_solution(4165918090907225273)
XLA Ops:
  7.2 1.2 fusion.20
  8.4 2.0 fusion.15
  10.5 1.8 convert_element_type.36
  12.4 0.7 all-gather.5.cloned.1.call-update
  13.1 46.2 %all-gather.9.cloned.1.call-done = bf16[1024,1024]{1,0:T(8,128)(2,1)} async-done(((bf16[256,1024]{1,0:T(8,128)(2,1)}), bf16[1024,1024]{1,0:T(8,128)(2,1)}) %all-gather.9.cloned.1.call-update) | async-done | bytes 2097168 | tf_op jit(solution)/shard_map/all_gather | solution.py:51
  59.3 29.1 %all-gather.11.cloned.1.call-done = bf16[1024,1024]{1,0:T(8,128)(2,1)} async-done(((bf16[128,1024]{1,0:T(8,128)(2,1)}), bf16[1024,1024]{1,0:T(8,128)(2,1)}) %all-gather.11.cloned.1.call-update) | async-done | bytes 2097168 | tf_op jit(solution)/shard_map/all_gather | solution.py:48
  88.4 6.5 %fusion.35 = f32[1024,1024]{1,0:T(8,128)} fusion(bf16[1024,1024]{1,0:T(8,128)(2,1)} %all-gather.9.cloned.1.call-done, bf16[1024,1024]{1,0:T(8,128)(2,1)} %all-gather.11.cloned.1.call-done), kind=kOutput, calls=%fused_computation.47 | convolution fusion | flops 2147483648 | bytes 8388608 | tf_op jit(solution)/shard_map/dot_general | solution.py:52
  94.9 41.0 %all-gather.5.cloned.1.call-done = bf16[1024,1024]{1,0:T(8,128)(2,1)} async-done(((bf16[256,1024]{1,0:T(8,128)(2,1)}), bf16[1024,1024]{1,0:T(8,128)(2,1)}) %all-gather.5.cloned.1.call-update) | async-done | bytes 2097168 | tf_op jit(solution)/shard_map/all_gather | solution.py:55
  135.9 5.6 %fusion.12 = bf16[1024,1024]{1,0:T(8,128)(2,1)S(1)} fusion(bf16[1024,1024]{1,0:T(8,128)(2,1)} %all-gather.5.cloned.1.call-done, f32[1024,1024]{1,0:T(8,128)} %fusion.35), kind=kOutput, calls=%fused_computation.15 | convolution fusion | flops 2157969408 | bytes 8388608 | tf_op jit(solution)/shard_map/dot_general | solution.py:38
  141.5 2.6 copy.15
  144.2 40.0 %reduce-scatter.10.cloned.1.call-done = bf16[128,1024]{1,0:T(8,128)(2,1)} async-done(((bf16[1024,1024]{1,0:T(8,128)(2,1)}), bf16[128,1024]{1,0:T(8,128)(2,1)}) %reduce-scatter.10.cloned.1.call-update) | async-done | bytes 262160
  184.2 1.1 copy.16
  185.3 2.5 multiply_subtract_fusion
  188.0 28.3 %all-gather.7.cloned.1.call-done = bf16[1024,1024]{1,0:T(8,128)(2,1)} async-done(((bf16[1024,128]{1,0:T(8,128)(2,1)}), bf16[1024,1024]{1,0:T(8,128)(2,1)}) %all-gather.7.cloned.1.call-update) | async-done | bytes 2097168 | tf_op jit(solution)/shard_map/all_gather | solution.py:49
  216.3 6.9 %fusion.6 = bf16[1024,1024]{1,0:T(8,128)(2,1)S(1)} fusion(f32[1024,1024]{1,0:T(8,128)} %fusion.35, bf16[1024,1024]{1,0:T(8,128)(2,1)S(1)} %copy-done.7, bf16[1024,1024]{1,0:T(8,128)(2,1)} %all-gather.7.cloned.1.call-done), kind=kOutput, calls=%fused_computation.8 | convolution fusion | flops 2168455168 | bytes 10485760 | tf_op jit(solution)/shard_map/dot_general | solution.py:57
  223.2 1.3 copy-done.8
  224.5 5.5 %convolution_convert_fusion = bf16[1024,1024]{1,0:T(8,128)(2,1)} fusion(bf16[1024,1024]{1,0:T(8,128)(2,1)} %all-gather.9.cloned.1.call-done, bf16[1024,1024]{1,0:T(8,128)(2,1)S(1)} %fusion.6), kind=kOutput, calls=%fused_computation.16 | convolution fusion | flops 2148532224 | bytes 6291456 | tf_op jit(solution)/shard_map/dot_general | solution.py:38
  230.1 0.2 reduce-scatter.6.cloned.1.call-start
  230.3 5.9 %fusion.36 = f32[1024,1024]{1,0:T(8,128)} fusion(bf16[1024,1024]{1,0:T(8,128)(2,1)} %copy-done.8, bf16[1024,1024]{1,0:T(8,128)(2,1)S(1)} %copy-done.6), kind=kOutput, calls=%fused_computation.48 | convolution fusion | flops 2147483648 | bytes 8388608 | tf_op jit(solution)/shard_map/dot_general | solution.py:71
  236.3 35.2 %reduce-scatter.8.cloned.1.call-done = bf16[128,1024]{1,0:T(8,128)(2,1)} async-done(((bf16[1024,1024]{1,0:T(8,128)(2,1)}), bf16[128,1024]{1,0:T(8,128)(2,1)}) %reduce-scatter.8.cloned.1.call-update) | async-done | bytes 262160 | tf_op jit(solution)/shard_map/reduce_scatter | solution.py:63
  271.5 2.4 multiply_subtract_fusion.1
  273.8 76.7 %reduce-scatter.6.cloned.1.call-done = f32[256,1024]{1,0:T(8,128)} async-done(((f32[1024,1024]{1,0:T(8,128)}), f32[256,1024]{1,0:T(8,128)}) %reduce-scatter.6.cloned.1.call-update) | async-done | bytes 1048592 | tf_op jit(solution)/shard_map/reduce_scatter | solution.py:70
  350.5 1.5 fusion.16
  352.1 2.3 fusion.19
  (31 shorter events, 0.4 us)
Async XLA Ops:
  7.2 52.1 %all-gather.9.cloned.1.call-start = ((), (), s32[]{:S(2)}) async-start(), calls=%async_computation.5 | async-start | bytes 2621440 | tf_op jit(solution)/shard_map/all_gather | solution.py:51
  10.5 77.9 %all-gather.11.cloned.1.call-start = ((), (), s32[]{:S(2)}) async-start(), calls=%async_computation.6 | async-start | bytes 2359296 | tf_op jit(solution)/shard_map/all_gather | solution.py:48
  12.3 123.6 %all-gather.5.cloned.1.call-start = ((), (), s32[]{:S(2)}) async-start(), calls=%async_computation.3 | async-start | bytes 2621440 | tf_op jit(solution)/shard_map/all_gather | solution.py:55
  13.1 171.1 %reduce-scatter.10.cloned.1.call-start = ((), (), s32[]{:S(2)}) async-start(), calls=%async_computation.9 | async-start | bytes 2359296
  141.5 43.8 %copy-start.2 = (f32[1024,128]{1,0:T(8,128)S(1)}, f32[1024,128]{1,0:T(8,128)}, u32[]{:S(2)}) copy-start(f32[1024,128]{1,0:T(8,128)} %param.11) | copy-start | bytes 1572868
  141.5 43.8 %copy-start.3 = (f32[1024,128]{1,0:T(8,128)S(1)}, f32[1024,128]{1,0:T(8,128)}, u32[]{:S(2)}) copy-start(f32[1024,128]{1,0:T(8,128)} %param.15) | copy-start | bytes 1572868
  144.1 72.2 %copy-start.7 = (bf16[1024,1024]{1,0:T(8,128)(2,1)S(1)}, bf16[1024,1024]{1,0:T(8,128)(2,1)}, u32[]{:S(2)}) copy-start(bf16[1024,1024]{1,0:T(8,128)(2,1)} %all-gather.5.cloned.1.call-done) | copy-start | bytes 6291460
  144.1 72.1 %all-gather.7.cloned.1.call-start = ((), (), s32[]{:S(2)}) async-start(), calls=%async_computation.4 | async-start | bytes 2359296 | tf_op jit(solution)/shard_map/all_gather | solution.py:49
  187.9 83.6 %reduce-scatter.8.cloned.1.call-start = ((), (), s32[]{:S(2)}) async-start(), calls=%async_computation.8 | async-start | bytes 2359296 | tf_op jit(solution)/shard_map/reduce_scatter | solution.py:63
  223.2 1.3 copy-start.8
  224.5 5.8 %copy-start.6 = (bf16[1024,1024]{1,0:T(8,128)(2,1)S(1)}, bf16[1024,1024]{1,0:T(8,128)(2,1)}, u32[]{:S(2)}) copy-start(bf16[1024,1024]{1,0:T(8,128)(2,1)} %all-gather.11.cloned.1.call-done) | copy-start | bytes 6291460
  230.1 120.5 %reduce-scatter.6.cloned.1.call-start = ((), (), s32[]{:S(2)}) async-start(), calls=%async_computation.7 | async-start | bytes 5242880 | tf_op jit(solution)/shard_map/reduce_scatter | solution.py:70
  236.2 35.2 %copy-start.1 = (f32[128,1024]{1,0:T(8,128)S(1)}, f32[128,1024]{1,0:T(8,128)}, u32[]{:S(2)}) copy-start(f32[128,1024]{1,0:T(8,128)} %param.10) | copy-start | bytes 1572868
  236.2 35.2 %copy-start.4 = (f32[128,1024]{1,0:T(8,128)S(1)}, f32[128,1024]{1,0:T(8,128)}, u32[]{:S(2)}) copy-start(f32[128,1024]{1,0:T(8,128)} %param.13) | copy-start | bytes 1572868
  236.2 35.2 %copy-start.5 = (f32[128,1024]{1,0:T(8,128)S(1)}, f32[128,1024]{1,0:T(8,128)}, u32[]{:S(2)}) copy-start(f32[128,1024]{1,0:T(8,128)} %param.12) | copy-start | bytes 1572868
  236.3 114.3 %copy-start = (bf16[256,1024]{1,0:T(8,128)(2,1)S(1)}, bf16[256,1024]{1,0:T(8,128)(2,1)}, u32[]{:S(2)}) copy-start(bf16[256,1024]{1,0:T(8,128)(2,1)} %param.8) | copy-start | bytes 1572868
Sparse Core Ops, SparseCore 0:
  10.6 48.6 all-gather.8
  61.7 26.5 all-gather.10
  89.9 45.9 all-gather.4
  144.2 39.9 reduce-scatter.9
  188.0 28.1 all-gather.6
  230.2 41.2 reduce-scatter.7
  273.8 76.7 reduce-scatter.5
where the time goes:
time: 362 us; the launch traced here: 361 us
  waiting for transfers between devices  297 us (82%)
  matrix products  30.5 us (8%)
  between operations  14.2 us (4%)
  other arithmetic  13.7 us (4%)
  local copies, waits for them, and re-layouts  5.04 us (1%)
    reduce_scatter x1, waiting for transfers between devices, shards(): lax.psum_scatter(lax.dot_general(d_preact, weight_in_b, (((1,), (1,)), ((...  76.7 us
    all_gather x1, waiting for transfers between devices, shards(): normed = lax.all_gather(normed_local, 'mp', axis=0, tiled=True)  46.2 us
    all_gather x1, waiting for transfers between devices, shards(): upstream = lax.all_gather(cotangent, 'mp', axis=0, tiled=True)  41 us
    unnamed x8, waiting for transfers between devices  40.8 us
    reduce_scatter x1, waiting for transfers between devices, shards(): lax.psum_scatter(in_partial.astype(jnp.bfloat16), 'dp', scatter_dimension...  35.2 us
    all_gather x1, waiting for transfers between devices, shards(): lax.all_gather(pieces[0], 'dp', axis=0, tiled=True)  29.1 us
    all_gather x1, waiting for transfers between devices, shards(): lax.all_gather(pieces[1], 'dp', axis=1, tiled=True)  28.3 us
    dot_general x2, matrix products, contract_rows(): lax.dot_general(left, right, (((0,), (0,)), ((), ())), preferred_element_...  11.1 us
  transfers between devices with their start and end apart: 7, of which 7 were waited for; matrix products, arithmetic and copies ran while one was open for 5% of the time, Pallas kernels for 0%

commit v1 on v0

v1 whole, which is shorter than its diff:
```python
import functools
import math

import jax
import jax.numpy as jnp
from jax import lax
from jax.experimental import pallas as pl
from jax.experimental.pallas import tpu as pltpu
from jax.sharding import PartitionSpec as P

MESH = pl.DeviceIdType.MESH
STEP = 1000

BETA_ONE = 0.9
BETA_TWO = 0.999
EPSILON = 1e-08
LEARN_RATE = 0.001
DECAY_RATE = 0.1
CUBIC = 0.044715
ROOT = math.sqrt(2.0 / math.pi)


def adam_step(weight, moment, second, gradient):
    moment_new = BETA_ONE * moment + (1.0 - BETA_ONE) * gradient
    second_new = BETA_TWO * second + (1.0 - BETA_TWO) * gradient * gradient
    first_fix = 1.0 - BETA_ONE ** float(STEP)
    second_fix = 1.0 - BETA_TWO ** float(STEP)
    update = moment_new / first_fix / (jnp.sqrt(second_new / second_fix) + EPSILON)
    weight_new = weight - LEARN_RATE * (update + DECAY_RATE * weight)
    return (weight_new, moment_new, second_new)


def gelu_pair(v):
    square = v * v
    t = jnp.tanh(ROOT * (v + CUBIC * (square * v)))
    half = 0.5 * (1.0 + t)
    slope = half + (0.5 * ROOT) * v * (1.0 - t * t) * (1.0 + (3.0 * CUBIC) * square)
    return v * half, slope


def kernel(
    n_dp, n_mp, tile,
    tokens_ref, cot_ref, win_ref, wout_ref,
    ig_ref, gin_ref, gout_ref,
    held, weights, grads, flipped, dn, ret_out, ret_in, sib_out, sib_in, chip_out, chip_in,
    tok_send, tok_recv, w_send, w_sib, w_recv, ret_send, ret_recv, sib_send, sib_recv, chip_send, chip_recv,
):
    n_chip = n_dp // 2
    dp, z = lax.axis_index("dp"), lax.axis_index("mp")
    chip, core = dp // 2, dp % 2
    sibling = chip * 2 + (1 - core)
    rows = win_ref.shape[0]
    hidden_units = win_ref.shape[1]
    f32, b16 = jnp.float32, jnp.bfloat16

    def other_chip(i):
        return (chip + i) % n_chip

    barrier = pltpu.get_barrier_semaphore()
    pl.semaphore_signal(barrier, inc=1, device_id=(sibling, z), device_id_type=MESH)
    for i in range(1, n_chip):
        pl.semaphore_signal(barrier, inc=1, device_id=(other_chip(i) * 2 + core, z), device_id_type=MESH)
    for i in range(1, n_mp):
        pl.semaphore_signal(barrier, inc=1, device_id=(dp, (z + i) % n_mp), device_id_type=MESH)

    values = tokens_ref[...].astype(f32)
    inverse = lax.rsqrt(jnp.mean(values * values, axis=-1, keepdims=True) + 1e-06)
    held[z, 0] = (values * inverse).astype(b16)
    held[z, 1] = cot_ref[...]
    own_rows = pl.ds(pl.multiple_of(dp * rows, rows), rows)
    weights[0, own_rows, :] = win_ref[...].astype(b16)
    weights[1, own_rows, :] = wout_ref[...].T.astype(b16)
    pl.semaphore_wait(barrier, n_chip + n_mp - 1)

    def tok_copy(origin, side, target):
        return pltpu.make_async_remote_copy(
            src_ref=held.at[origin], dst_ref=held.at[origin],
            send_sem=tok_send.at[side, origin], recv_sem=tok_recv.at[origin],
            device_id=(dp, target), device_id_type=MESH)

    def weight_copy(owner, send_sem, target):
        block = weights.at[:, pl.ds(pl.multiple_of(owner * rows, rows), rows), :]
        return pltpu.make_async_remote_copy(
            src_ref=block, dst_ref=block, send_sem=send_sem, recv_sem=w_recv.at[owner],
            device_id=(target, z), device_id_type=MESH)

    def ret_copy(origin):
        return pltpu.make_async_remote_copy(
            src_ref=ret_out.at[origin], dst_ref=ret_in.at[z],
            send_sem=ret_send.at[origin], recv_sem=ret_recv.at[z],
            device_id=(dp, origin), device_id_type=MESH)

    def ret_arrival(sender):
        return pltpu.make_async_remote_copy(
            src_ref=ret_in.at[sender], dst_ref=ret_in.at[sender],
            send_sem=ret_send.at[sender], recv_sem=ret_recv.at[sender],
            device_id=(dp, sender), device_id_type=MESH)

    def sib_copy(k):
        return pltpu.make_async_remote_copy(
            src_ref=sib_out.at[k], dst_ref=sib_in.at[k],
            send_sem=sib_send.at[k], recv_sem=sib_recv.at[k],
            device_id=(sibling, z), device_id_type=MESH)

    def chip_copy(k):
        return pltpu.make_async_remote_copy(
            src_ref=chip_out.at[k], dst_ref=chip_in.at[chip],
            send_sem=chip_send.at[k], recv_sem=chip_recv.at[chip],
            device_id=(k * 2 + core, z), device_id_type=MESH)

    def chip_arrival(k):
        return pltpu.make_async_remote_copy(
            src_ref=chip_in.at[k], dst_ref=chip_in.at[k],
            send_sem=chip_send.at[k], recv_sem=chip_recv.at[k],
            device_id=(k * 2 + core, z), device_id_type=MESH)

    @pl.when(z < n_mp - 1)
    def _():
        tok_copy(z, 0, z + 1).start()

    @pl.when(z > 0)
    def _():
        tok_copy(z, 1, z - 1).start()

    for i in range(1, n_chip):
        k = other_chip(i)
        weight_copy(dp, w_send.at[k], k * 2 + core).start()
    weight_copy(dp, w_sib.at[chip], sibling).start()

    def clear(i, carry):
        part = pl.ds(pl.multiple_of(i * rows, rows), rows)
        grads[:, part, :] = jnp.zeros((2, rows, hidden_units), f32)
        return carry

    lax.fori_loop(0, n_dp, clear, 0)

    for i in range(1, n_chip):
        owner = other_chip(i) * 2 + core
        weight_copy(owner, w_sib.at[other_chip(i)], sibling).wait_recv()
        weight_copy(owner, w_sib.at[other_chip(i)], sibling).start()

    def pass_on(distance):
        @pl.when(z - distance >= 0)
        def _():
            tok_copy(z - distance, 0, z).wait_recv()

            @pl.when(z < n_mp - 1)
            def _():
                tok_copy(z - distance, 0, z + 1).start()

        @pl.when(z + distance < n_mp)
        def _():
            tok_copy(z + distance, 1, z).wait_recv()

            @pl.when(z > 0)
            def _():
                tok_copy(z + distance, 1, z - 1).start()

    pass_on(1)
    for k in range(n_chip):
        weight_copy(k * 2 + (1 - core), w_sib.at[k], sibling).wait_recv()

    at_end = (z == 0) | (z == n_mp - 1)

    def chunk(origin):
        flipped[0] = held[origin, 0].T
        flipped[1] = held[origin, 1].T

        def columns(step, carry):
            part = pl.ds(pl.multiple_of(step * tile, tile), tile)
            w_in = weights[0, :, part]
            preact = jnp.dot(held[origin, 0], w_in, preferred_element_type=f32)
            d_hidden = jnp.dot(held[origin, 1], weights[1, :, part], preferred_element_type=f32)
            hidden, slope = gelu_pair(preact)
            d_preact = (d_hidden * slope).astype(b16)
            grads[0, :, part] += jnp.dot(flipped[0], d_preact, preferred_element_type=f32)
            grads[1, :, part] += jnp.dot(flipped[1], hidden.astype(b16), preferred_element_type=f32)
            back = lax.dot_general(d_preact, w_in, (((1,), (1,)), ((), ())), preferred_element_type=f32)

            @pl.when(step == 0)
            def _():
                dn[...] = back

            @pl.when(step > 0)
            def _():
                dn[...] += back
            return carry

        lax.fori_loop(0, hidden_units // tile, columns, 0)

        @pl.when(origin == z)
        def _():
            ig_ref[...] = dn[...]

        @pl.when(origin != z)
        def _():
            ret_out[origin] = dn[...].astype(b16)

            @pl.when(at_end)
            def _():
                ret_copy(origin).start()

    def at_distance(distance, carry):
        @pl.when(distance >= 2)
        def _():
            pass_on(distance)

        def side(which, inner):
            origin = z + distance * (2 * which - 1)

            @pl.when((origin >= 0) & (origin < n_mp) & (distance + which > 0))
            def _():
                chunk(jnp.where(distance == 0, z, origin))
            return inner

        lax.fori_loop(jnp.where(distance == 0, 1, 0), 2, side, 0)
        return carry

    lax.fori_loop(0, n_mp, at_distance, 0)

    def block(owner):
        return grads[:, pl.ds(pl.multiple_of(owner * rows, rows), rows), :]

    for i in range(n_chip):
        k = other_chip(i + 1)
        sib_out[k] = block(k * 2 + (1 - core)).astype(b16)
        sib_copy(k).start()
    for i in range(1, n_chip):
        k = other_chip(i)
        sib_copy(k).wait_recv()
        chip_out[k] = (block(k * 2 + core) + sib_in[k].astype(f32)).astype(b16)
        chip_copy(k).start()

    for origin in range(n_mp):
        @pl.when((z < n_mp - 1) & (origin <= z))
        def _():
            tok_copy(origin, 0, z + 1).wait_send()

        @pl.when((z > 0) & (origin >= z))
        def _():
            tok_copy(origin, 1, z - 1).wait_send()
    for origin in range(n_mp):
        @pl.when((origin != z) & jnp.logical_not(at_end))
        def _():
            ret_copy(origin).start()

    sib_copy(chip).wait_recv()
    total = block(dp) + sib_in[chip].astype(f32)
    for i in range(1, n_chip):
        k = other_chip(i)
        chip_arrival(k).wait_recv()
        total += chip_in[k].astype(f32)
    gin_ref[...] = total[0]
    gout_ref[...] = total[1].T

    for i in range(1, n_mp):
        sender = (z + i) % n_mp
        ret_arrival(sender).wait_recv()
        ig_ref[...] += ret_in[sender].astype(f32)
    values = tokens_ref[...].astype(f32)
    inverse = lax.rsqrt(jnp.mean(values * values, axis=-1, keepdims=True) + 1e-06)
    normed = values * inverse
    d_normed = ig_ref[...]
    ig_ref[...] = inverse * (d_normed - normed * jnp.mean(d_normed * normed, axis=-1, keepdims=True))

    for i in range(1, n_chip):
        k = other_chip(i)
        weight_copy(dp, w_send.at[k], k * 2 + core).wait_send()
        chip_copy(k).wait_send()
    for k in range(n_chip):
        weight_copy(k * 2 + core, w_sib.at[k], sibling).wait_send()
        sib_copy(k).wait_send()
    for i in range(1, n_mp):
        ret_copy((z + i) % n_mp).wait_send()


def shards(n_dp, n_mp, tokens, cotangent, weight_in, weight_out, moment_in, second_in, moment_out, second_out):
    count, width = tokens.shape
    rows, units = weight_in.shape
    n_chip = n_dp // 2
    b16, f32 = jnp.bfloat16, jnp.float32
    vmem = pl.BlockSpec(memory_space=pltpu.VMEM)
    dma = pltpu.SemaphoreType.DMA
    flops = 10 * count * n_mp * width * units
    d_rows, grad_in, grad_out = pl.pallas_call(
        functools.partial(kernel, n_dp, n_mp, min(256, units)),
        out_shape=(
            jax.ShapeDtypeStruct((count, width), f32),
            jax.ShapeDtypeStruct((rows, units), f32),
            jax.ShapeDtypeStruct((units, rows), f32),
        ),
        in_specs=[vmem] * 4,
        out_specs=(vmem,) * 3,
        scratch_shapes=[
            pltpu.VMEM((n_mp, 2, count, width), b16),
            pltpu.VMEM((2, width, units), b16),
            pltpu.VMEM((2, width, units), f32),
            pltpu.VMEM((2, width, count), b16),
            pltpu.VMEM((count, width), f32),
            pltpu.VMEM((n_mp, count, width), b16),
            pltpu.VMEM((n_mp, count, width), b16),
            pltpu.VMEM((n_chip, 2, rows, units), b16),
            pltpu.VMEM((n_chip, 2, rows, units), b16),
            pltpu.VMEM((n_chip, 2, rows, units), b16),
            pltpu.VMEM((n_chip, 2, rows, units), b16),
            dma((2, n_mp)), dma((n_mp,)),
            dma((n_chip,)), dma((n_chip,)), dma((n_dp,)),
            dma((n_mp,)), dma((n_mp,)),
            dma((n_chip,)), dma((n_chip,)),
            dma((n_chip,)), dma((n_chip,)),
        ],
        compiler_params=pltpu.CompilerParams(
            collective_id=0, has_side_effects=True, vmem_limit_bytes=56 * 1024 * 1024
        ),
        cost_estimate=pl.CostEstimate(flops=flops, bytes_accessed=8 * rows * units * 4, transcendentals=0),
    )(tokens, cotangent, weight_in, weight_out)
    input_grad = d_rows.astype(b16)
    grad_scale = 1.0 / jnp.sqrt(jnp.float32(count * n_dp * n_mp))
    new_in = adam_step(weight_in, moment_in, second_in, grad_in * grad_scale)
    new_out = adam_step(weight_out, moment_out, second_out, grad_out * grad_scale)
    return (input_grad, *new_in, *new_out)


def solution(mesh):
    return jax.shard_map(
        functools.partial(shards, mesh.shape["dp"], mesh.shape["mp"]),
        mesh=mesh,
        in_specs=(
            P(("dp", "mp"), None),
            P(("dp", "mp"), None),
            P("dp", "mp"),
            P("mp", "dp"),
            P("dp", "mp"),
            P("dp", "mp"),
            P("mp", "dp"),
            P("mp", "dp"),
        ),
        out_specs=(
            P(("dp", "mp"), None),
            P("dp", "mp"),
            P("dp", "mp"),
            P("dp", "mp"),
            P("mp", "dp"),
            P("mp", "dp"),
            P("mp", "dp"),
        ),
        check_vma=False,
    )
```

time: 362 us -> 141 us (0.39)
  waiting for transfers between devices: 297 us -> 0 us
  Pallas kernels: 0 us -> 133 us
  matrix products: 30.5 us -> 0 us
  between operations: 14.2 us -> 0.71 us
  other arithmetic: 13.7 us -> 6.18 us
  local copies, waits for them, and re-layouts: 5.04 us -> 0.04 us
    all_gather x4 -> x0, waiting for transfers between devices: 145 us -> none  [the longest x1 46.2 us: shards(): normed = lax.all_gather(normed_local, 'mp', axis=0, tiled=True)]
    pallas_call x0 -> x1, Pallas kernels: none -> 133 us  [shards(): pl.pallas_call(functools.partial(kernel, n_dp, n_mp, min(256, units)), ou...]
    reduce_scatter x2 -> x0, waiting for transfers between devices: 112 us -> none  [the longest x1 76.7 us: shards(): lax.psum_scatter(lax.dot_general(d_preact, weight_in_b, (((1,), (1,)), ((...]
    unnamed x8 -> x0, waiting for transfers between devices: 40.8 us -> none
    dot_general x5 -> x0, matrix products: 30.5 us -> none  [the longest x2 11.1 us: contract_rows(): lax.dot_general(left, right, (((0,), (0,)), ((), ())), preferred_element_...]
    unnamed x20 -> x14, local copies, waits for them, and re-layouts: 5.04 us -> 0.04 us
    convert_element_type x3 -> x1, other arithmetic: 6.05 us -> 2.21 us  [shards(): input_grad = d_rows.astype(b16)]
  transfers between devices with their start and end apart: 7 -> 0, of which waited for: 7 -> 0; matrix products, arithmetic and copies ran while one was open for 5% -> 0% of each run, Pallas kernels for 0% -> 0%
where the time goes in v1:
time: 141 us; the launch traced here: 140 us
  Pallas kernels  133 us (94%)
  other arithmetic  6.18 us (4%)
    pallas_call x1, Pallas kernels, shards(): pl.pallas_call(functools.partial(kernel, n_dp, n_mp, min(256, units)), ou...  133 us
    sub x2, other arithmetic, adam_step(): weight_new = weight - LEARN_RATE * (update + DECAY_RATE * weight)  3.98 us

profile of v1, /device:TPU:0, one launch (start us, length us, event | category | flops | bytes accessed | tf_op | source)
XLA Modules:
  0.0 139.9 jit_solution(453682316484124271)
XLA Ops:
  0.6 132.9 %shard_map.135 = (f32[256,1024]{1,0:T(8,128)}, f32[128,1024]{1,0:T(8,128)}, f32[1024,128]{1,0:T(8,128)}) custom-call(bf16[256,1024]{1,0:T(8,128)(2,1)} %tokens_ref.1, bf16[256,1024]{1,0:T(8,128)(2,1)} %cot_ref.1, f32[128,1024]{1,0:T(8,128)} %win_ref.1, f32[1024,128]{1,0:T(8,128)} %wout_ref.1), custom_call_target="tpu_custom_call" | custom-call | flops 10737418240 | bytes 4194304 | tf_op jit(solution)/shard_map/pallas_call | solution.py:285
  133.6 0.0 copy-start
  133.6 0.0 copy-start.1
  133.6 0.0 copy-start.2
  133.6 2.2 %convert_element_type.3 = bf16[256,1024]{1,0:T(8,128)(2,1)} convert(f32[256,1024]{1,0:T(8,128)} %get-tuple-element.10) | non-fusion elementwise | flops 262144 | bytes 1572864 | tf_op jit(solution)/shard_map/convert_element_type | solution.py:317
  135.8 0.0 copy-done
  135.8 0.0 copy-done.1
  135.8 0.0 copy-done.2
  135.8 0.0 copy-start.3
  135.8 0.0 copy-start.4
  135.9 0.0 copy-start.5
  135.9 0.0 copy-start.6
  135.9 2.6 %multiply_subtract_fusion.1 = (f32[128,1024]{1,0:T(8,128)}, f32[128,1024]{1,0:T(8,128)}, f32[128,1024]{1,0:T(8,128)}) fusion(f32[128,1024]{1,0:T(8,128)S(1)} %copy-done, f32[128,1024]{1,0:T(8,128)} %get-tuple-element.11, f32[128,1024]{1,0:T(8,128)S(1)} %copy-done.1, f32[128,1024]{1,0:T(8,128)S(1)} %copy-done.2), kind=kLoop, calls=%fused_computation.3 | loop fusion | flops 1966080 | bytes 3670016 | tf_op jit(solution)/shard_map/sub | solution.py:29
  138.5 0.0 copy-done.3
  138.5 0.0 copy-done.4
  138.5 0.0 copy-done.5
  138.5 0.0 copy-done.6
  138.5 1.4 multiply_subtract_fusion
Async XLA Ops:
  133.6 2.2 %copy-start = (f32[128,1024]{1,0:T(8,128)S(1)}, f32[128,1024]{1,0:T(8,128)}, u32[]{:S(2)}) copy-start(f32[128,1024]{1,0:T(8,128)} %win_ref.1) | copy-start | bytes 1572868
  133.6 2.2 %copy-start.1 = (f32[128,1024]{1,0:T(8,128)S(1)}, f32[128,1024]{1,0:T(8,128)}, u32[]{:S(2)}) copy-start(f32[128,1024]{1,0:T(8,128)} %param.13) | copy-start | bytes 1572868
  133.6 2.2 %copy-start.2 = (f32[128,1024]{1,0:T(8,128)S(1)}, f32[128,1024]{1,0:T(8,128)}, u32[]{:S(2)}) copy-start(f32[128,1024]{1,0:T(8,128)} %param.12) | copy-start | bytes 1572868
  135.8 2.6 %copy-start.3 = (f32[1024,128]{1,0:T(8,128)S(1)}, f32[1024,128]{1,0:T(8,128)}, u32[]{:S(2)}) copy-start(f32[1024,128]{1,0:T(8,128)} %wout_ref.1) | copy-start | bytes 1572868
  135.8 2.6 %copy-start.4 = (f32[1024,128]{1,0:T(8,128)S(1)}, f32[1024,128]{1,0:T(8,128)}, u32[]{:S(2)}) copy-start(f32[1024,128]{1,0:T(8,128)} %param.15) | copy-start | bytes 1572868
  135.9 2.6 %copy-start.5 = (f32[1024,128]{1,0:T(8,128)S(1)}, f32[1024,128]{1,0:T(8,128)}, u32[]{:S(2)}) copy-start(f32[1024,128]{1,0:T(8,128)} %param.14) | copy-start | bytes 1572868
  135.9 2.6 %copy-start.6 = (f32[1024,128]{1,0:T(8,128)S(1)}, f32[1024,128]{1,0:T(8,128)}, u32[]{:S(2)}) copy-start(f32[1024,128]{1,0:T(8,128)} %get-tuple-element.12) | copy-start | bytes 1572868

commit v2 on v1

v2 whole, which is shorter than its diff:
```python
import functools
import math

import jax
import jax.numpy as jnp
from jax import lax
from jax.experimental import pallas as pl
from jax.experimental.pallas import tpu as pltpu
from jax.sharding import PartitionSpec as P

MESH = pl.DeviceIdType.MESH
STEP = 1000

BETA_ONE = 0.9
BETA_TWO = 0.999
EPSILON = 1e-08
LEARN_RATE = 0.001
DECAY_RATE = 0.1
CUBIC = 0.044715
ROOT = math.sqrt(2.0 / math.pi)


def adam_step(weight, moment, second, gradient):
    moment_new = BETA_ONE * moment + (1.0 - BETA_ONE) * gradient
    second_new = BETA_TWO * second + (1.0 - BETA_TWO) * gradient * gradient
    first_fix = 1.0 - BETA_ONE ** float(STEP)
    second_fix = 1.0 - BETA_TWO ** float(STEP)
    update = moment_new / first_fix / (jnp.sqrt(second_new / second_fix) + EPSILON)
    weight_new = weight - LEARN_RATE * (update + DECAY_RATE * weight)
    return (weight_new, moment_new, second_new)


def gelu_pair(v):
    square = v * v
    t = jnp.tanh(ROOT * (v + CUBIC * (square * v)))
    half = 0.5 * (1.0 + t)
    slope = half + (0.5 * ROOT) * v * (1.0 - t * t) * (1.0 + (3.0 * CUBIC) * square)
    return v * half, slope


def kernel(
    n_dp, n_mp, tile,
    tokens_ref, cot_ref, win_ref, wout_ref,
    ig_ref, gin_ref, gout_ref,
    held, weights, grads, flipped, dn, own, ret_out, ret_in, sib_out, sib_in, chip_out, chip_in,
    tok_send, tok_recv, w_send, w_sib, w_recv, ret_send, ret_recv, sib_send, sib_recv, chip_send, chip_recv,
):
    n_chip = n_dp // 2
    dp, z = lax.axis_index("dp"), lax.axis_index("mp")
    chip, core = dp // 2, dp % 2
    sibling = chip * 2 + (1 - core)
    rows = win_ref.shape[0]
    hidden_units = win_ref.shape[1]
    f32, b16 = jnp.float32, jnp.bfloat16
    n_tile = hidden_units // tile
    n_ret = ret_send.shape[1]
    ret_rows = tokens_ref.shape[0] // n_ret

    def other_chip(i):
        return (chip + i) % n_chip

    barrier = pltpu.get_barrier_semaphore()
    pl.semaphore_signal(barrier, inc=1, device_id=(sibling, z), device_id_type=MESH)
    for i in range(1, n_chip):
        pl.semaphore_signal(barrier, inc=1, device_id=(other_chip(i) * 2 + core, z), device_id_type=MESH)
    for i in range(1, n_mp):
        pl.semaphore_signal(barrier, inc=1, device_id=(dp, (z + i) % n_mp), device_id_type=MESH)

    values = tokens_ref[...].astype(f32)
    inverse = lax.rsqrt(jnp.mean(values * values, axis=-1, keepdims=True) + 1e-06)
    held[z, 0] = (values * inverse).astype(b16)
    held[z, 1] = cot_ref[...]
    own_rows = pl.ds(pl.multiple_of(dp * rows, rows), rows)
    weights[0, own_rows, :] = win_ref[...].astype(b16)
    weights[1, own_rows, :] = wout_ref[...].T.astype(b16)
    pl.semaphore_wait(barrier, n_chip + n_mp - 1)

    def tok_copy(origin, piece, side, target):
        return pltpu.make_async_remote_copy(
            src_ref=held.at[origin, piece], dst_ref=held.at[origin, piece],
            send_sem=tok_send.at[side, origin, piece], recv_sem=tok_recv.at[origin, piece],
            device_id=(dp, target), device_id_type=MESH)

    def weight_copy(owner, send_sem, target):
        block = weights.at[:, pl.ds(pl.multiple_of(owner * rows, rows), rows), :]
        return pltpu.make_async_remote_copy(
            src_ref=block, dst_ref=block, send_sem=send_sem, recv_sem=w_recv.at[owner],
            device_id=(target, z), device_id_type=MESH)

    def ret_copy(target, step, way):
        part = pl.ds(step * ret_rows, ret_rows)
        slot = jnp.where((z + way == target) & (way == 1), n_mp, target)
        return pltpu.make_async_remote_copy(
            src_ref=ret_out.at[target, part], dst_ref=ret_in.at[slot, part],
            send_sem=ret_send.at[target, step], recv_sem=ret_recv.at[slot, step],
            device_id=(dp, z + way), device_id_type=MESH)

    def ret_arrival(slot, step):
        part = pl.ds(step * ret_rows, ret_rows)
        return pltpu.make_async_remote_copy(
            src_ref=ret_in.at[slot, part], dst_ref=ret_in.at[slot, part],
            send_sem=ret_send.at[0, step], recv_sem=ret_recv.at[slot, step],
            device_id=(dp, z), device_id_type=MESH)

    def sib_copy(t):
        return pltpu.make_async_remote_copy(
            src_ref=sib_out.at[t], dst_ref=sib_in.at[t],
            send_sem=sib_send.at[t], recv_sem=sib_recv.at[t],
            device_id=(sibling, z), device_id_type=MESH)

    def chip_copy(t, k):
        return pltpu.make_async_remote_copy(
            src_ref=chip_out.at[t, k], dst_ref=chip_in.at[t, chip],
            send_sem=chip_send.at[t, k], recv_sem=chip_recv.at[t, chip],
            device_id=(k * 2 + core, z), device_id_type=MESH)

    def chip_arrival(t, k):
        return pltpu.make_async_remote_copy(
            src_ref=chip_in.at[t, k], dst_ref=chip_in.at[t, k],
            send_sem=chip_send.at[t, k], recv_sem=chip_recv.at[t, k],
            device_id=(k * 2 + core, z), device_id_type=MESH)

    def block(owner, t):
        return grads[:, pl.ds(pl.multiple_of(owner * rows, rows), rows), pl.ds(pl.multiple_of(t * tile, tile), tile)]

    def core_stage(t):
        for k in range(n_chip):
            sib_out[t, k] = block(k * 2 + (1 - core), t).astype(b16)
        sib_copy(t).start()

    def chip_stage(t):
        sib_copy(t).wait_recv()
        for i in range(1, n_chip):
            k = other_chip(i)
            chip_out[t, k] = (block(k * 2 + core, t) + sib_in[t, k].astype(f32)).astype(b16)
            chip_copy(t, k).start()

    @pl.when(z < n_mp - 1)
    def _():
        for piece in range(2):
            tok_copy(z, piece, 0, z + 1).start()

    @pl.when(z > 0)
    def _():
        for piece in range(2):
            tok_copy(z, piece, 1, z - 1).start()

    for i in range(1, n_chip):
        k = other_chip(i)
        weight_copy(dp, w_send.at[k], k * 2 + core).start()
    weight_copy(dp, w_sib.at[chip], sibling).start()

    def clear(i, carry):
        part = pl.ds(pl.multiple_of(i * rows, rows), rows)
        grads[:, part, :] = jnp.zeros((2, rows, hidden_units), f32)
        return carry

    lax.fori_loop(0, n_dp, clear, 0)

    for i in range(1, n_chip):
        owner = other_chip(i) * 2 + core
        weight_copy(owner, w_sib.at[other_chip(i)], sibling).wait_recv()
        weight_copy(owner, w_sib.at[other_chip(i)], sibling).start()

    def pass_on(distance):
        for piece in range(2):
            @pl.when(z - distance >= 0)
            def _():
                tok_copy(z - distance, piece, 0, z).wait_recv()

                @pl.when(z < n_mp - 1)
                def _():
                    tok_copy(z - distance, piece, 0, z + 1).start()

            @pl.when(z + distance < n_mp)
            def _():
                tok_copy(z + distance, piece, 1, z).wait_recv()

                @pl.when(z > 0)
                def _():
                    tok_copy(z + distance, piece, 1, z - 1).start()

    pass_on(1)
    for k in range(n_chip):
        weight_copy(k * 2 + (1 - core), w_sib.at[k], sibling).wait_recv()

    furthest = jnp.where(z > n_mp - 1 - z, z, n_mp - 1 - z)
    at_end = (z == 0) | (z == n_mp - 1)

    def chunk(origin, last):
        flipped[0] = held[origin, 0].T
        flipped[1] = held[origin, 1].T

        def columns(step, carry):
            part = pl.ds(pl.multiple_of(step * tile, tile), tile)
            w_in = weights[0, :, part]
            preact = jnp.dot(held[origin, 0], w_in, preferred_element_type=f32)
            d_hidden = jnp.dot(held[origin, 1], weights[1, :, part], preferred_element_type=f32)
            hidden, slope = gelu_pair(preact)
            d_preact = (d_hidden * slope).astype(b16)
            grads[0, :, part] += jnp.dot(flipped[0], d_preact, preferred_element_type=f32)
            grads[1, :, part] += jnp.dot(flipped[1], hidden.astype(b16), preferred_element_type=f32)
            back = lax.dot_general(d_preact, w_in, (((1,), (1,)), ((), ())), preferred_element_type=f32)

            @pl.when(step == 0)
            def _():
                dn[...] = back

            @pl.when(step > 0)
            def _():
                dn[...] += back

            @pl.when(last)
            def _():
                core_stage(step)

                @pl.when(step > 0)
                def _():
                    chip_stage(step - 1)
            return carry

        lax.fori_loop(0, n_tile, columns, 0)

        @pl.when(origin == z)
        def _():
            own[...] = dn[...]

        @pl.when(origin != z)
        def _():
            ret_out[origin] = dn[...].astype(b16)

            @pl.when(at_end)
            def _():
                for step in range(n_ret):
                    ret_copy(origin, step, jnp.where(z == 0, 1, -1)).start()

    def at_distance(distance, carry):
        @pl.when(distance >= 2)
        def _():
            pass_on(distance)

        def side(which, inner):
            origin = z + distance * (2 * which - 1)

            @pl.when((origin >= 0) & (origin < n_mp) & (distance + which > 0))
            def _():
                chunk(origin, (distance == furthest) & ((which == 1) | (z + distance >= n_mp)))
            return inner

        lax.fori_loop(jnp.where(distance == 0, 1, 0), 2, side, 0)
        return carry

    lax.fori_loop(0, n_mp, at_distance, 0)

    chip_stage(n_tile - 1)

    def hand_on(far, carry):
        for step in range(n_ret):
            for turn in range(2):
                down = (turn + z // (n_mp // 2)) % 2
                way = 1 - 2 * down
                target = far + down * (n_mp - 1 - 2 * far)

                @pl.when(((target - z) * way > 0) & jnp.logical_not(at_end))
                def _():
                    part = pl.ds(step * ret_rows, ret_rows)
                    ret_arrival(target, step).wait_recv()
                    ret_out[target, part] = (
                        ret_out[target, part].astype(f32) + ret_in[target, part].astype(f32)
                    ).astype(b16)
                    ret_copy(target, step, way).start()
        return carry

    lax.fori_loop(1, n_mp, hand_on, 0)

    for t in range(n_tile):
        total = block(dp, t) + sib_in[t, chip].astype(f32)
        for i in range(1, n_chip):
            k = other_chip(i)
            chip_arrival(t, k).wait_recv()
            total += chip_in[t, k].astype(f32)
        gin_ref[:, t * tile:(t + 1) * tile] = total[0]
        gout_ref[t * tile:(t + 1) * tile, :] = total[1].T

    @pl.when(z < n_mp - 1)
    def _():
        for step in range(n_ret):
            ret_arrival(z, step).wait_recv()
        own[...] += ret_in[z].astype(f32)

    @pl.when(z > 0)
    def _():
        for step in range(n_ret):
            ret_arrival(n_mp, step).wait_recv()
        own[...] += ret_in[n_mp].astype(f32)

    values = tokens_ref[...].astype(f32)
    inverse = lax.rsqrt(jnp.mean(values * values, axis=-1, keepdims=True) + 1e-06)
    normed = values * inverse
    d_normed = own[...]
    d_rows = inverse * (d_normed - normed * jnp.mean(d_normed * normed, axis=-1, keepdims=True))
    ig_ref[...] = d_rows.astype(b16)

    for i in range(1, n_chip):
        k = other_chip(i)
        weight_copy(dp, w_send.at[k], k * 2 + core).wait_send()
        for t in range(n_tile):
            chip_copy(t, k).wait_send()
    for k in range(n_chip):
        weight_copy(k * 2 + core, w_sib.at[k], sibling).wait_send()
    for t in range(n_tile):
        sib_copy(t).wait_send()
    for origin in range(n_mp):
        for piece in range(2):
            @pl.when((z < n_mp - 1) & (origin <= z))
            def _():
                tok_copy(origin, piece, 0, z + 1).wait_send()

            @pl.when((z > 0) & (origin >= z))
            def _():
                tok_copy(origin, piece, 1, z - 1).wait_send()
    for i in range(1, n_mp):
        target = (z + i) % n_mp
        for step in range(n_ret):
            ret_copy(target, step, jnp.where(target > z, 1, -1)).wait_send()


def shards(n_dp, n_mp, tokens, cotangent, weight_in, weight_out, moment_in, second_in, moment_out, second_out):
    count, width = tokens.shape
    rows, units = weight_in.shape
    n_chip = n_dp // 2
    n_ret = 4
    tile = min(256, units)
    n_tile = units // tile
    b16, f32 = jnp.bfloat16, jnp.float32
    vmem = pl.BlockSpec(memory_space=pltpu.VMEM)
    dma = pltpu.SemaphoreType.DMA
    flops = 10 * count * n_mp * width * units
    input_grad, grad_in, grad_out = pl.pallas_call(
        functools.partial(kernel, n_dp, n_mp, tile),
        out_shape=(
            jax.ShapeDtypeStruct((count, width), b16),
            jax.ShapeDtypeStruct((rows, units), f32),
            jax.ShapeDtypeStruct((units, rows), f32),
        ),
        in_specs=[vmem] * 4,
        out_specs=(vmem,) * 3,
        scratch_shapes=[
            pltpu.VMEM((n_mp, 2, count, width), b16),
            pltpu.VMEM((2, width, units), b16),
            pltpu.VMEM((2, width, units), f32),
            pltpu.VMEM((2, width, count), b16),
            pltpu.VMEM((count, width), f32),
            pltpu.VMEM((count, width), f32),
            pltpu.VMEM((n_mp, count, width), b16),
            pltpu.VMEM((n_mp + 1, count, width), b16),
            pltpu.VMEM((n_tile, n_chip, 2, rows, tile), b16),
            pltpu.VMEM((n_tile, n_chip, 2, rows, tile), b16),
            pltpu.VMEM((n_tile, n_chip, 2, rows, tile), b16),
            pltpu.VMEM((n_tile, n_chip, 2, rows, tile), b16),
            dma((2, n_mp, 2)), dma((n_mp, 2)),
            dma((n_chip,)), dma((n_chip,)), dma((n_dp,)),
            dma((n_mp, n_ret)), dma((n_mp + 1, n_ret)),
            dma((n_tile,)), dma((n_tile,)),
            dma((n_tile, n_chip)), dma((n_tile, n_chip)),
        ],
        compiler_params=pltpu.CompilerParams(
            collective_id=0, has_side_effects=True, vmem_limit_bytes=56 * 1024 * 1024
        ),
        cost_estimate=pl.CostEstimate(flops=flops, bytes_accessed=8 * rows * units * 4, transcendentals=0),
    )(tokens, cotangent, weight_in, weight_out)
    grad_scale = 1.0 / jnp.sqrt(jnp.float32(count * n_dp * n_mp))
    new_in = adam_step(weight_in, moment_in, second_in, grad_in * grad_scale)
    new_out = adam_step(weight_out, moment_out, second_out, grad_out * grad_scale)
    return (input_grad, *new_in, *new_out)


def solution(mesh):
    return jax.shard_map(
        functools.partial(shards, mesh.shape["dp"], mesh.shape["mp"]),
        mesh=mesh,
        in_specs=(
            P(("dp", "mp"), None),
            P(("dp", "mp"), None),
            P("dp", "mp"),
            P("mp", "dp"),
            P("dp", "mp"),
            P("dp", "mp"),
            P("mp", "dp"),
            P("mp", "dp"),
        ),
        out_specs=(
            P(("dp", "mp"), None),
            P("dp", "mp"),
            P("dp", "mp"),
            P("dp", "mp"),
            P("mp", "dp"),
            P("mp", "dp"),
            P("mp", "dp"),
        ),
        check_vma=False,
    )
```

time: 141 us -> 119 us (0.84)
  Pallas kernels: 133 us -> 113 us
  other arithmetic: 6.18 us -> 3.98 us
    pallas_call x1, Pallas kernels: 133 us -> 113 us  [shards(): pl.pallas_call(functools.partial(kernel, n_dp, n_mp, tile), out_shape=(ja...]
    convert_element_type x1 -> x0, other arithmetic: 2.21 us -> none  [shards(): input_grad = d_rows.astype(b16)]
where the time goes in v2:
time: 119 us
  Pallas kernels  113 us (95%)
  other arithmetic  3.98 us (3%)
    pallas_call x1, Pallas kernels, shards(): pl.pallas_call(functools.partial(kernel, n_dp, n_mp, tile), out_shape=(ja...  113 us
    sub x2, other arithmetic, adam_step(): weight_new = weight - LEARN_RATE * (update + DECAY_RATE * weight)  3.98 us

profile of v2, /device:TPU:0, one launch (start us, length us, event | category | flops | bytes accessed | tf_op | source)
XLA Modules:
  0.0 118.7 jit_solution(16500079317412365952)
XLA Ops:
  0.6 0.0 copy-start
  0.6 0.0 copy-start.1
  0.7 0.0 copy-start.2
  0.7 113.1 %shard_map.135 = (bf16[256,1024]{1,0:T(8,128)(2,1)}, f32[128,1024]{1,0:T(8,128)}, f32[1024,128]{1,0:T(8,128)}) custom-call(bf16[256,1024]{1,0:T(8,128)(2,1)} %tokens_ref.1, bf16[256,1024]{1,0:T(8,128)(2,1)} %cot_ref.1, f32[128,1024]{1,0:T(8,128)} %win_ref.1, f32[1024,128]{1,0:T(8,128)} %wout_ref.1), custom_call_target="tpu_custom_call" | custom-call | flops 10737418240 | bytes 4194304 | tf_op jit(solution)/shard_map/pallas_call | solution.py:339
  113.8 0.0 copy-done
  113.8 0.0 copy-done.1
  113.8 0.0 copy-done.2
  113.8 0.0 copy-start.3
  113.8 0.0 copy-start.4
  113.9 0.0 copy-start.5
  113.9 0.0 copy-start.6
  113.9 2.6 %multiply_subtract_fusion.1 = (f32[128,1024]{1,0:T(8,128)}, f32[128,1024]{1,0:T(8,128)}, f32[128,1024]{1,0:T(8,128)}) fusion(f32[128,1024]{1,0:T(8,128)S(1)} %copy-done, f32[128,1024]{1,0:T(8,128)} %get-tuple-element.11, f32[128,1024]{1,0:T(8,128)S(1)} %copy-done.1, f32[128,1024]{1,0:T(8,128)S(1)} %copy-done.2), kind=kLoop, calls=%fused_computation.3 | loop fusion | flops 1966080 | bytes 3670016 | tf_op jit(solution)/shard_map/sub | solution.py:29
  116.5 0.0 copy-done.3
  116.5 0.0 copy-done.4
  116.5 0.0 copy-done.5
  116.5 0.0 copy-done.6
  116.5 0.0 copy-start.7
  116.5 1.4 %multiply_subtract_fusion = (f32[1024,128]{1,0:T(8,128)}, f32[1024,128]{1,0:T(8,128)}, f32[1024,128]{1,0:T(8,128)}) fusion(f32[1024,128]{1,0:T(8,128)S(1)} %copy-done.3, f32[1024,128]{1,0:T(8,128)S(1)} %copy-done.6, f32[1024,128]{1,0:T(8,128)S(1)} %copy-done.4, f32[1024,128]{1,0:T(8,128)S(1)} %copy-done.5), kind=kLoop, calls=%fused_computation | loop fusion | flops 1966080 | bytes 3670016 | tf_op jit(solution)/shard_map/sub | solution.py:29
  117.9 0.0 copy-done.7
  117.9 0.8 copy.16
Async XLA Ops:
  0.6 113.2 %copy-start = (f32[128,1024]{1,0:T(8,128)S(1)}, f32[128,1024]{1,0:T(8,128)}, u32[]{:S(2)}) copy-start(f32[128,1024]{1,0:T(8,128)} %win_ref.1) | copy-start | bytes 1572868
  0.6 113.2 %copy-start.1 = (f32[128,1024]{1,0:T(8,128)S(1)}, f32[128,1024]{1,0:T(8,128)}, u32[]{:S(2)}) copy-start(f32[128,1024]{1,0:T(8,128)} %param.13) | copy-start | bytes 1572868
  0.7 113.2 %copy-start.2 = (f32[128,1024]{1,0:T(8,128)S(1)}, f32[128,1024]{1,0:T(8,128)}, u32[]{:S(2)}) copy-start(f32[128,1024]{1,0:T(8,128)} %param.12) | copy-start | bytes 1572868
  113.8 2.7 %copy-start.3 = (f32[1024,128]{1,0:T(8,128)S(1)}, f32[1024,128]{1,0:T(8,128)}, u32[]{:S(2)}) copy-start(f32[1024,128]{1,0:T(8,128)} %wout_ref.1) | copy-start | bytes 1572868
  113.8 2.6 %copy-start.4 = (f32[1024,128]{1,0:T(8,128)S(1)}, f32[1024,128]{1,0:T(8,128)}, u32[]{:S(2)}) copy-start(f32[1024,128]{1,0:T(8,128)} %param.15) | copy-start | bytes 1572868
  113.9 2.6 %copy-start.5 = (f32[1024,128]{1,0:T(8,128)S(1)}, f32[1024,128]{1,0:T(8,128)}, u32[]{:S(2)}) copy-start(f32[1024,128]{1,0:T(8,128)} %param.14) | copy-start | bytes 1572868
  113.9 2.6 %copy-start.6 = (f32[1024,128]{1,0:T(8,128)S(1)}, f32[1024,128]{1,0:T(8,128)}, u32[]{:S(2)}) copy-start(f32[1024,128]{1,0:T(8,128)} %get-tuple-element.12) | copy-start | bytes 1572868
  116.5 1.4 %copy-start.7 = (bf16[256,1024]{1,0:T(8,128)(2,1)S(1)}, bf16[256,1024]{1,0:T(8,128)(2,1)}, u32[]{:S(2)}) copy-start(bf16[256,1024]{1,0:T(8,128)(2,1)} %get-tuple-element.26) | copy-start | bytes 1572868

commit v3 on v2

--- a/solution.py
+++ b/solution.py
@@ -66,15 +66,6 @@
     for i in range(1, n_mp):
         pl.semaphore_signal(barrier, inc=1, device_id=(dp, (z + i) % n_mp), device_id_type=MESH)
 
-    values = tokens_ref[...].astype(f32)
-    inverse = lax.rsqrt(jnp.mean(values * values, axis=-1, keepdims=True) + 1e-06)
-    held[z, 0] = (values * inverse).astype(b16)
-    held[z, 1] = cot_ref[...]
-    own_rows = pl.ds(pl.multiple_of(dp * rows, rows), rows)
-    weights[0, own_rows, :] = win_ref[...].astype(b16)
-    weights[1, own_rows, :] = wout_ref[...].T.astype(b16)
-    pl.semaphore_wait(barrier, n_chip + n_mp - 1)
-
     def tok_copy(origin, piece, side, target):
         return pltpu.make_async_remote_copy(
             src_ref=held.at[origin, piece], dst_ref=held.at[origin, piece],
@@ -135,20 +126,29 @@
             chip_out[t, k] = (block(k * 2 + core, t) + sib_in[t, k].astype(f32)).astype(b16)
             chip_copy(t, k).start()
 
-    @pl.when(z < n_mp - 1)
-    def _():
-        for piece in range(2):
+    def send_own(piece):
+        @pl.when(z < n_mp - 1)
+        def _():
             tok_copy(z, piece, 0, z + 1).start()
 
-    @pl.when(z > 0)
-    def _():
-        for piece in range(2):
+        @pl.when(z > 0)
+        def _():
             tok_copy(z, piece, 1, z - 1).start()
 
+    held[z, 1] = cot_ref[...]
+    own_rows = pl.ds(pl.multiple_of(dp * rows, rows), rows)
+    weights[0, own_rows, :] = win_ref[...].astype(b16)
+    weights[1, own_rows, :] = wout_ref[...].T.astype(b16)
+    pl.semaphore_wait(barrier, n_chip + n_mp - 1)
+    send_own(1)
     for i in range(1, n_chip):
         k = other_chip(i)
         weight_copy(dp, w_send.at[k], k * 2 + core).start()
     weight_copy(dp, w_sib.at[chip], sibling).start()
+    values = tokens_ref[...].astype(f32)
+    inverse = lax.rsqrt(jnp.mean(values * values, axis=-1, keepdims=True) + 1e-06)
+    held[z, 0] = (values * inverse).astype(b16)
+    send_own(0)
 
     def clear(i, carry):
         part = pl.ds(pl.multiple_of(i * rows, rows), rows)
@@ -163,7 +163,7 @@
         weight_copy(owner, w_sib.at[other_chip(i)], sibling).start()
 
     def pass_on(distance):
-        for piece in range(2):
+        for piece in (1, 0):
             @pl.when(z - distance >= 0)
             def _():
                 tok_copy(z - distance, piece, 0, z).wait_recv()
@@ -180,12 +180,16 @@
                 def _():
                     tok_copy(z + distance, piece, 1, z - 1).start()
 
-    pass_on(1)
+    at_end = (z == 0) | (z == n_mp - 1)
+
+    @pl.when(jnp.logical_not(at_end))
+    def _():
+        pass_on(1)
+
     for k in range(n_chip):
         weight_copy(k * 2 + (1 - core), w_sib.at[k], sibling).wait_recv()
 
     furthest = jnp.where(z > n_mp - 1 - z, z, n_mp - 1 - z)
-    at_end = (z == 0) | (z == n_mp - 1)
 
     def chunk(origin, last):
         flipped[0] = held[origin, 0].T
@@ -235,9 +239,11 @@
                     ret_copy(origin, step, jnp.where(z == 0, 1, -1)).start()
 
     def at_distance(distance, carry):
-        @pl.when(distance >= 2)
+        ahead = distance + jnp.where(at_end, 0, 1)
+
+        @pl.when((distance >= 1) & (ahead < n_mp))
         def _():
-            pass_on(distance)
+            pass_on(ahead)
 
         def side(which, inner):
             origin = z + distance * (2 * which - 1)
@@ -329,7 +335,7 @@
     count, width = tokens.shape
     rows, units = weight_in.shape
     n_chip = n_dp // 2
-    n_ret = 4
+    n_ret = 8
     tile = min(256, units)
     n_tile = units // tile
     b16, f32 = jnp.bfloat16, jnp.float32

time: 119 us -> 127 us (1.067)
  Pallas kernels: 113 us -> 121 us
    pallas_call x1, Pallas kernels: 113 us -> 121 us  [shards(): pl.pallas_call(functools.partial(kernel, n_dp, n_mp, tile), out_shape=(ja...]
where the time goes in v3:
time: 127 us; the launch traced here: 126 us
  Pallas kernels  121 us (95%)
  other arithmetic  3.98 us (3%)
    pallas_call x1, Pallas kernels, shards(): pl.pallas_call(functools.partial(kernel, n_dp, n_mp, tile), out_shape=(ja...  121 us
    sub x2, other arithmetic, adam_step(): weight_new = weight - LEARN_RATE * (update + DECAY_RATE * weight)  3.98 us

profile of v3, /device:TPU:0, one launch (start us, length us, event | category | flops | bytes accessed | tf_op | source)
XLA Modules:
  0.0 126.4 jit_solution(14444263213080369706)
XLA Ops:
  0.6 0.0 copy-start
  0.6 0.0 copy-start.1
  0.7 0.0 copy-start.2
  0.7 120.8 %shard_map.135 = (bf16[256,1024]{1,0:T(8,128)(2,1)}, f32[128,1024]{1,0:T(8,128)}, f32[1024,128]{1,0:T(8,128)}) custom-call(bf16[256,1024]{1,0:T(8,128)(2,1)} %tokens_ref.1, bf16[256,1024]{1,0:T(8,128)(2,1)} %cot_ref.1, f32[128,1024]{1,0:T(8,128)} %win_ref.1, f32[1024,128]{1,0:T(8,128)} %wout_ref.1), custom_call_target="tpu_custom_call" | custom-call | flops 10737418240 | bytes 4194304 | tf_op jit(solution)/shard_map/pallas_call | solution.py:345
  121.5 0.0 copy-done
  121.5 0.0 copy-done.1
  121.5 0.0 copy-done.2
  121.5 0.0 copy-start.3
  121.5 0.0 copy-start.4
  121.5 0.0 copy-start.5
  121.5 0.0 copy-start.6
  121.5 2.6 %multiply_subtract_fusion.1 = (f32[128,1024]{1,0:T(8,128)}, f32[128,1024]{1,0:T(8,128)}, f32[128,1024]{1,0:T(8,128)}) fusion(f32[128,1024]{1,0:T(8,128)S(1)} %copy-done, f32[128,1024]{1,0:T(8,128)} %get-tuple-element.11, f32[128,1024]{1,0:T(8,128)S(1)} %copy-done.1, f32[128,1024]{1,0:T(8,128)S(1)} %copy-done.2), kind=kLoop, calls=%fused_computation.3 | loop fusion | flops 1966080 | bytes 3670016 | tf_op jit(solution)/shard_map/sub | solution.py:29
  124.2 0.0 copy-done.3
  124.2 0.0 copy-done.4
  124.2 0.0 copy-done.5
  124.2 0.0 copy-done.6
  124.2 0.0 copy-start.7
  124.2 1.4 %multiply_subtract_fusion = (f32[1024,128]{1,0:T(8,128)}, f32[1024,128]{1,0:T(8,128)}, f32[1024,128]{1,0:T(8,128)}) fusion(f32[1024,128]{1,0:T(8,128)S(1)} %copy-done.3, f32[1024,128]{1,0:T(8,128)S(1)} %copy-done.6, f32[1024,128]{1,0:T(8,128)S(1)} %copy-done.4, f32[1024,128]{1,0:T(8,128)S(1)} %copy-done.5), kind=kLoop, calls=%fused_computation | loop fusion | flops 1966080 | bytes 3670016 | tf_op jit(solution)/shard_map/sub | solution.py:29
  125.6 0.0 copy-done.7
  125.6 0.8 copy.16
Async XLA Ops:
  0.6 120.8 %copy-start = (f32[128,1024]{1,0:T(8,128)S(1)}, f32[128,1024]{1,0:T(8,128)}, u32[]{:S(2)}) copy-start(f32[128,1024]{1,0:T(8,128)} %win_ref.1) | copy-start | bytes 1572868
  0.6 120.8 %copy-start.1 = (f32[128,1024]{1,0:T(8,128)S(1)}, f32[128,1024]{1,0:T(8,128)}, u32[]{:S(2)}) copy-start(f32[128,1024]{1,0:T(8,128)} %param.13) | copy-start | bytes 1572868
  0.7 120.8 %copy-start.2 = (f32[128,1024]{1,0:T(8,128)S(1)}, f32[128,1024]{1,0:T(8,128)}, u32[]{:S(2)}) copy-start(f32[128,1024]{1,0:T(8,128)} %param.12) | copy-start | bytes 1572868
  121.5 2.7 %copy-start.3 = (f32[1024,128]{1,0:T(8,128)S(1)}, f32[1024,128]{1,0:T(8,128)}, u32[]{:S(2)}) copy-start(f32[1024,128]{1,0:T(8,128)} %wout_ref.1) | copy-start | bytes 1572868
  121.5 2.6 %copy-start.4 = (f32[1024,128]{1,0:T(8,128)S(1)}, f32[1024,128]{1,0:T(8,128)}, u32[]{:S(2)}) copy-start(f32[1024,128]{1,0:T(8,128)} %param.15) | copy-start | bytes 1572868
  121.5 2.6 %copy-start.5 = (f32[1024,128]{1,0:T(8,128)S(1)}, f32[1024,128]{1,0:T(8,128)}, u32[]{:S(2)}) copy-start(f32[1024,128]{1,0:T(8,128)} %param.14) | copy-start | bytes 1572868
  121.5 2.6 %copy-start.6 = (f32[1024,128]{1,0:T(8,128)S(1)}, f32[1024,128]{1,0:T(8,128)}, u32[]{:S(2)}) copy-start(f32[1024,128]{1,0:T(8,128)} %get-tuple-element.12) | copy-start | bytes 1572868
  124.2 1.4 %copy-start.7 = (bf16[256,1024]{1,0:T(8,128)(2,1)S(1)}, bf16[256,1024]{1,0:T(8,128)(2,1)}, u32[]{:S(2)}) copy-start(bf16[256,1024]{1,0:T(8,128)(2,1)} %get-tuple-element.26) | copy-start | bytes 1572868

commit v4 on v3

--- a/solution.py
+++ b/solution.py
@@ -30,6 +30,16 @@
     return (weight_new, moment_new, second_new)
 
 
+def update(scale, ig_ref, *refs):
+    gin, win, min_, sin, gout, wout, mout, sout, ig_new, *new = refs
+    ig_new[...] = ig_ref[...]
+    for place, group in ((0, (win, min_, sin, gin)), (3, (wout, mout, sout, gout))):
+        weight, moment, second, gradient = (ref[...] for ref in group)
+        results = adam_step(weight, moment, second, gradient * scale)
+        for offset, result in enumerate(results):
+            new[place + offset][...] = result
+
+
 def gelu_pair(v):
     square = v * v
     t = jnp.tanh(ROOT * (v + CUBIC * (square * v)))
@@ -42,7 +52,7 @@
     n_dp, n_mp, tile,
     tokens_ref, cot_ref, win_ref, wout_ref,
     ig_ref, gin_ref, gout_ref,
-    held, weights, grads, flipped, dn, own, ret_out, ret_in, sib_out, sib_in, chip_out, chip_in,
+    held, weights, grads, flipped, win_t, d_pre, own, ret_out, ret_in, sib_out, sib_in, chip_out, chip_in,
     tok_send, tok_recv, w_send, w_sib, w_recv, ret_send, ret_recv, sib_send, sib_recv, chip_send, chip_recv,
 ):
     n_chip = n_dp // 2
@@ -53,6 +63,9 @@
     hidden_units = win_ref.shape[1]
     f32, b16 = jnp.float32, jnp.bfloat16
     n_tile = hidden_units // tile
+    width = tokens_ref.shape[1]
+    wide = min(256, width)
+    n_wide = width // wide
     n_ret = ret_send.shape[1]
     ret_rows = tokens_ref.shape[0] // n_ret
 
@@ -182,12 +195,16 @@
 
     at_end = (z == 0) | (z == n_mp - 1)
 
-    @pl.when(jnp.logical_not(at_end))
-    def _():
-        pass_on(1)
-
+    pass_on(1)
     for k in range(n_chip):
         weight_copy(k * 2 + (1 - core), w_sib.at[k], sibling).wait_recv()
+
+    def turn(step, carry):
+        part = pl.ds(pl.multiple_of(step * wide, wide), wide)
+        win_t[:, part] = weights[0, part, :].T
+        return carry
+
+    lax.fori_loop(0, n_wide, turn, 0)
 
     furthest = jnp.where(z > n_mp - 1 - z, z, n_mp - 1 - z)
 
@@ -197,22 +214,13 @@
 
         def columns(step, carry):
             part = pl.ds(pl.multiple_of(step * tile, tile), tile)
-            w_in = weights[0, :, part]
-            preact = jnp.dot(held[origin, 0], w_in, preferred_element_type=f32)
+            preact = jnp.dot(held[origin, 0], weights[0, :, part], preferred_element_type=f32)
             d_hidden = jnp.dot(held[origin, 1], weights[1, :, part], preferred_element_type=f32)
             hidden, slope = gelu_pair(preact)
             d_preact = (d_hidden * slope).astype(b16)
             grads[0, :, part] += jnp.dot(flipped[0], d_preact, preferred_element_type=f32)
             grads[1, :, part] += jnp.dot(flipped[1], hidden.astype(b16), preferred_element_type=f32)
-            back = lax.dot_general(d_preact, w_in, (((1,), (1,)), ((), ())), preferred_element_type=f32)
-
-            @pl.when(step == 0)
-            def _():
-                dn[...] = back
-
-            @pl.when(step > 0)
-            def _():
-                dn[...] += back
+            d_pre[:, part] = d_preact
 
             @pl.when(last)
             def _():
@@ -225,25 +233,32 @@
 
         lax.fori_loop(0, n_tile, columns, 0)
 
-        @pl.when(origin == z)
-        def _():
-            own[...] = dn[...]
+        def back(step, carry):
+            part = pl.ds(pl.multiple_of(step * wide, wide), wide)
+            sums = jnp.dot(d_pre[...], win_t[:, part], preferred_element_type=f32)
+
+            @pl.when(origin == z)
+            def _():
+                own[:, part] = sums
+
+            @pl.when(origin != z)
+            def _():
+                ret_out[origin, :, part] = sums.astype(b16)
+            return carry
+
+        lax.fori_loop(0, n_wide, back, 0)
 
         @pl.when(origin != z)
         def _():
-            ret_out[origin] = dn[...].astype(b16)
-
             @pl.when(at_end)
             def _():
                 for step in range(n_ret):
                     ret_copy(origin, step, jnp.where(z == 0, 1, -1)).start()
 
     def at_distance(distance, carry):
-        ahead = distance + jnp.where(at_end, 0, 1)
-
-        @pl.when((distance >= 1) & (ahead < n_mp))
+        @pl.when(distance >= 2)
         def _():
-            pass_on(ahead)
+            pass_on(distance)
 
         def side(which, inner):
             origin = z + distance * (2 * which - 1)
@@ -335,7 +350,7 @@
     count, width = tokens.shape
     rows, units = weight_in.shape
     n_chip = n_dp // 2
-    n_ret = 8
+    n_ret = 4
     tile = min(256, units)
     n_tile = units // tile
     b16, f32 = jnp.bfloat16, jnp.float32
@@ -356,7 +371,8 @@
             pltpu.VMEM((2, width, units), b16),
             pltpu.VMEM((2, width, units), f32),
             pltpu.VMEM((2, width, count), b16),
-            pltpu.VMEM((count, width), f32),
+            pltpu.VMEM((units, width), b16),
+            pltpu.VMEM((count, units), b16),
             pltpu.VMEM((count, width), f32),
             pltpu.VMEM((n_mp, count, width), b16),
             pltpu.VMEM((n_mp + 1, count, width), b16),
@@ -375,10 +391,20 @@
         ),
         cost_estimate=pl.CostEstimate(flops=flops, bytes_accessed=8 * rows * units * 4, transcendentals=0),
     )(tokens, cotangent, weight_in, weight_out)
-    grad_scale = 1.0 / jnp.sqrt(jnp.float32(count * n_dp * n_mp))
-    new_in = adam_step(weight_in, moment_in, second_in, grad_in * grad_scale)
-    new_out = adam_step(weight_out, moment_out, second_out, grad_out * grad_scale)
-    return (input_grad, *new_in, *new_out)
+    n_step = 4
+    across = pl.BlockSpec((rows, units // n_step), lambda i: (0, i))
+    down = pl.BlockSpec((units // n_step, rows), lambda i: (i, 0))
+    token_rows = pl.BlockSpec((count // n_step, width), lambda i: (i, 0))
+    return pl.pallas_call(
+        functools.partial(update, 1.0 / math.sqrt(count * n_dp * n_mp)),
+        grid=(n_step,),
+        out_shape=(jax.ShapeDtypeStruct((count, width), b16),)
+        + (jax.ShapeDtypeStruct((rows, units), f32),) * 3
+        + (jax.ShapeDtypeStruct((units, rows), f32),) * 3,
+        in_specs=[token_rows] + [across] * 4 + [down] * 4,
+        out_specs=(token_rows,) + (across,) * 3 + (down,) * 3,
+        cost_estimate=pl.CostEstimate(flops=40 * rows * units, bytes_accessed=56 * rows * units, transcendentals=0),
+    )(input_grad, grad_in, weight_in, moment_in, second_in, grad_out, weight_out, moment_out, second_out)
 
 
 def solution(mesh):

time: 127 us -> 121 us (0.953)
  other arithmetic: 3.98 us -> 0 us
    pallas_call x1, Pallas kernels: 121 us -> 115 us  [shards(): pl.pallas_call(functools.partial(kernel, n_dp, n_mp, tile), out_shape=(ja...]
    pallas_call x0 -> x1, Pallas kernels: none -> 4.89 us  [shards(): pl.pallas_call(functools.partial(update, 1.0 / math.sqrt(count * n_dp * n...]
    sub x2 -> x0, other arithmetic: 3.98 us -> none  [adam_step(): weight_new = weight - LEARN_RATE * (update + DECAY_RATE * weight)]
where the time goes in v4:
time: 121 us; the launch traced here: 120 us
  Pallas kernels  120 us (99%)
    pallas_call x1, Pallas kernels, shards(): pl.pallas_call(functools.partial(kernel, n_dp, n_mp, tile), out_shape=(ja...  115 us
    pallas_call x1, Pallas kernels, shards(): pl.pallas_call(functools.partial(update, 1.0 / math.sqrt(count * n_dp * n...  4.89 us

profile of v4, /device:TPU:0, one launch (start us, length us, event | category | flops | bytes accessed | tf_op | source)
XLA Modules:
  0.0 120.3 jit_solution(5854728000532833180)
XLA Ops:
  0.6 114.8 %shard_map.135 = (bf16[256,1024]{1,0:T(8,128)(2,1)}, f32[128,1024]{1,0:T(8,128)}, f32[1024,128]{1,0:T(8,128)}) custom-call(bf16[256,1024]{1,0:T(8,128)(2,1)} %tokens_ref.1, bf16[256,1024]{1,0:T(8,128)(2,1)} %cot_ref.1, f32[128,1024]{1,0:T(8,128)} %refs_1_.1, f32[1024,128]{1,0:T(8,128)} %refs_5_.1), custom_call_target="tpu_custom_call" | custom-call | flops 10737418240 | bytes 4194304 | tf_op jit(solution)/shard_map/pallas_call | solution.py:360
  115.4 4.9 %shard_map.136 = (bf16[256,1024]{1,0:T(8,128)(2,1)}, f32[128,1024]{1,0:T(8,128)}, f32[128,1024]{1,0:T(8,128)}, f32[128,1024]{1,0:T(8,128)}, f32[1024,128]{1,0:T(...) custom-call(bf16[256,1024]{1,0:T(8,128)(2,1)} %get-tuple-element.10.ig_ref, f32[128,1024]{1,0:T(8,128)} %get-tuple-element.11.refs_0_, ...), custom_call_target="tpu_custom_call" | custom-call | flops 5242880 | bytes 7340032 | tf_op jit(solution)/shard_map/pallas_call | solution.py:398

commit v5 on v3

--- a/solution.py
+++ b/solution.py
@@ -43,7 +43,7 @@
     tokens_ref, cot_ref, win_ref, wout_ref,
     ig_ref, gin_ref, gout_ref,
     held, weights, grads, flipped, dn, own, ret_out, ret_in, sib_out, sib_in, chip_out, chip_in,
-    tok_send, tok_recv, w_send, w_sib, w_recv, ret_send, ret_recv, sib_send, sib_recv, chip_send, chip_recv,
+    tok_send, tok_recv, w_send, w_relay, w_sib, w_recv, ret_send, ret_recv, sib_send, sib_recv, chip_send, chip_recv,
 ):
     n_chip = n_dp // 2
     dp, z = lax.axis_index("dp"), lax.axis_index("mp")
@@ -72,11 +72,23 @@
             send_sem=tok_send.at[side, origin, piece], recv_sem=tok_recv.at[origin, piece],
             device_id=(dp, target), device_id_type=MESH)
 
-    def weight_copy(owner, send_sem, target):
-        block = weights.at[:, pl.ds(pl.multiple_of(owner * rows, rows), rows), :]
-        return pltpu.make_async_remote_copy(
-            src_ref=block, dst_ref=block, send_sem=send_sem, recv_sem=w_recv.at[owner],
+    def weight_copy(owner, piece, send_sem, target):
+        block = weights.at[piece, pl.ds(pl.multiple_of(owner * rows, rows), rows), :]
+        return pltpu.make_async_remote_copy(
+            src_ref=block, dst_ref=block, send_sem=send_sem, recv_sem=w_recv.at[owner, piece],
             device_id=(target, z), device_id_type=MESH)
+
+    square = n_chip == 4
+    near_x, near_y, diagonal = chip + 1 - 2 * (chip % 2), (chip + 2) % 4, 3 - chip
+    if square:
+        direct = [near_x, near_y]
+        arrivals = [
+            (near_x, 0, near_y), (near_y, 1, near_x), (near_x, 1, None),
+            (near_y, 0, None), (diagonal, 0, None), (diagonal, 1, None),
+        ]
+    else:
+        direct = [other_chip(i) for i in range(1, n_chip)]
+        arrivals = [(k, piece, None) for k in direct for piece in range(2)]
 
     def ret_copy(target, step, way):
         part = pl.ds(step * ret_rows, ret_rows)
@@ -99,20 +111,27 @@
             send_sem=sib_send.at[t], recv_sem=sib_recv.at[t],
             device_id=(sibling, z), device_id_type=MESH)
 
-    def chip_copy(t, k):
-        return pltpu.make_async_remote_copy(
-            src_ref=chip_out.at[t, k], dst_ref=chip_in.at[t, chip],
-            send_sem=chip_send.at[t, k], recv_sem=chip_recv.at[t, chip],
-            device_id=(k * 2 + core, z), device_id_type=MESH)
-
-    def chip_arrival(t, k):
-        return pltpu.make_async_remote_copy(
-            src_ref=chip_in.at[t, k], dst_ref=chip_in.at[t, k],
-            send_sem=chip_send.at[t, k], recv_sem=chip_recv.at[t, k],
-            device_id=(k * 2 + core, z), device_id_type=MESH)
-
-    def block(owner, t):
-        return grads[:, pl.ds(pl.multiple_of(owner * rows, rows), rows), pl.ds(pl.multiple_of(t * tile, tile), tile)]
+    def chip_copy(t, k, piece):
+        target, slot = k, chip
+        if k is diagonal and square:
+            target = near_y if piece else near_x
+            slot = 3 - target
+        return pltpu.make_async_remote_copy(
+            src_ref=chip_out.at[t, k, piece], dst_ref=chip_in.at[t, slot, piece],
+            send_sem=chip_send.at[t, k, piece], recv_sem=chip_recv.at[t, slot, piece],
+            device_id=(target * 2 + core, z), device_id_type=MESH)
+
+    def chip_arrival(t, k, piece):
+        return pltpu.make_async_remote_copy(
+            src_ref=chip_in.at[t, k, piece], dst_ref=chip_in.at[t, k, piece],
+            send_sem=chip_send.at[t, k, piece], recv_sem=chip_recv.at[t, k, piece],
+            device_id=(sibling, z), device_id_type=MESH)
+
+    def block(owner, t, piece=slice(None)):
+        return grads[piece, pl.ds(pl.multiple_of(owner * rows, rows), rows), pl.ds(pl.multiple_of(t * tile, tile), tile)]
+
+    def paired(t, k, piece):
+        return block(k * 2 + core, t, piece) + sib_in[t, k, piece].astype(f32)
 
     def core_stage(t):
         for k in range(n_chip):
@@ -121,10 +140,22 @@
 
     def chip_stage(t):
         sib_copy(t).wait_recv()
-        for i in range(1, n_chip):
-            k = other_chip(i)
-            chip_out[t, k] = (block(k * 2 + core, t) + sib_in[t, k].astype(f32)).astype(b16)
-            chip_copy(t, k).start()
+        if square:
+            sends = [(diagonal, 0), (diagonal, 1), (near_x, 0), (near_y, 1)]
+        else:
+            sends = [(k, piece) for k in direct for piece in range(2)]
+        for k, piece in sends:
+            chip_out[t, k, piece] = paired(t, k, piece).astype(b16)
+            chip_copy(t, k, piece).start()
+
+    def relay_stage(t):
+        if square:
+            for piece, k in enumerate((near_y, near_x)):
+                chip_arrival(t, diagonal, piece).wait_recv()
+                chip_out[t, k, piece] = (
+                    paired(t, k, piece) + chip_in[t, diagonal, piece].astype(f32)
+                ).astype(b16)
+                chip_copy(t, k, piece).start()
 
     def send_own(piece):
         @pl.when(z < n_mp - 1)
@@ -141,10 +172,10 @@
     weights[1, own_rows, :] = wout_ref[...].T.astype(b16)
     pl.semaphore_wait(barrier, n_chip + n_mp - 1)
     send_own(1)
-    for i in range(1, n_chip):
-        k = other_chip(i)
-        weight_copy(dp, w_send.at[k], k * 2 + core).start()
-    weight_copy(dp, w_sib.at[chip], sibling).start()
+    for piece in range(2):
+        for k in direct:
+            weight_copy(dp, piece, w_send.at[k, piece], k * 2 + core).start()
+        weight_copy(dp, piece, w_sib.at[chip, piece], sibling).start()
     values = tokens_ref[...].astype(f32)
     inverse = lax.rsqrt(jnp.mean(values * values, axis=-1, keepdims=True) + 1e-06)
     held[z, 0] = (values * inverse).astype(b16)
@@ -157,10 +188,11 @@
 
     lax.fori_loop(0, n_dp, clear, 0)
 
-    for i in range(1, n_chip):
-        owner = other_chip(i) * 2 + core
-        weight_copy(owner, w_sib.at[other_chip(i)], sibling).wait_recv()
-        weight_copy(owner, w_sib.at[other_chip(i)], sibling).start()
+    for k, piece, relay in arrivals:
+        weight_copy(k * 2 + core, piece, w_sib.at[k, piece], sibling).wait_recv()
+        if relay is not None:
+            weight_copy(k * 2 + core, piece, w_relay.at[piece], relay * 2 + core).start()
+        weight_copy(k * 2 + core, piece, w_sib.at[k, piece], sibling).start()
 
     def pass_on(distance):
         for piece in (1, 0):
@@ -182,12 +214,10 @@
 
     at_end = (z == 0) | (z == n_mp - 1)
 
-    @pl.when(jnp.logical_not(at_end))
-    def _():
-        pass_on(1)
-
+    pass_on(1)
     for k in range(n_chip):
-        weight_copy(k * 2 + (1 - core), w_sib.at[k], sibling).wait_recv()
+        for piece in range(2):
+            weight_copy(k * 2 + (1 - core), piece, w_sib.at[k, piece], sibling).wait_recv()
 
     furthest = jnp.where(z > n_mp - 1 - z, z, n_mp - 1 - z)
 
@@ -221,6 +251,10 @@
                 @pl.when(step > 0)
                 def _():
                     chip_stage(step - 1)
+
+                @pl.when(step > 1)
+                def _():
+                    relay_stage(step - 2)
             return carry
 
         lax.fori_loop(0, n_tile, columns, 0)
@@ -239,13 +273,13 @@
                     ret_copy(origin, step, jnp.where(z == 0, 1, -1)).start()
 
     def at_distance(distance, carry):
-        ahead = distance + jnp.where(at_end, 0, 1)
-
-        @pl.when((distance >= 1) & (ahead < n_mp))
-        def _():
-            pass_on(ahead)
-
         def side(which, inner):
+            ahead = distance + which
+
+            @pl.when((ahead >= 2) & (ahead < n_mp) & (which == jnp.where(at_end, 0, 1)))
+            def _():
+                pass_on(ahead)
+
             origin = z + distance * (2 * which - 1)
 
             @pl.when((origin >= 0) & (origin < n_mp) & (distance + which > 0))
@@ -259,6 +293,8 @@
     lax.fori_loop(0, n_mp, at_distance, 0)
 
     chip_stage(n_tile - 1)
+    for t in range(max(0, n_tile - 2), n_tile):
+        relay_stage(t)
 
     def hand_on(far, carry):
         for step in range(n_ret):
@@ -280,13 +316,15 @@
     lax.fori_loop(1, n_mp, hand_on, 0)
 
     for t in range(n_tile):
-        total = block(dp, t) + sib_in[t, chip].astype(f32)
-        for i in range(1, n_chip):
-            k = other_chip(i)
-            chip_arrival(t, k).wait_recv()
-            total += chip_in[t, k].astype(f32)
-        gin_ref[:, t * tile:(t + 1) * tile] = total[0]
-        gout_ref[t * tile:(t + 1) * tile, :] = total[1].T
+        totals = []
+        for piece in range(2):
+            total = paired(t, chip, piece)
+            for k in direct:
+                chip_arrival(t, k, piece).wait_recv()
+                total += chip_in[t, k, piece].astype(f32)
+            totals.append(total)
+        gin_ref[:, t * tile:(t + 1) * tile] = totals[0]
+        gout_ref[t * tile:(t + 1) * tile, :] = totals[1].T
 
     @pl.when(z < n_mp - 1)
     def _():
@@ -307,13 +345,17 @@
     d_rows = inverse * (d_normed - normed * jnp.mean(d_normed * normed, axis=-1, keepdims=True))
     ig_ref[...] = d_rows.astype(b16)
 
-    for i in range(1, n_chip):
-        k = other_chip(i)
-        weight_copy(dp, w_send.at[k], k * 2 + core).wait_send()
+    for piece in range(2):
+        for k in direct:
+            weight_copy(dp, piece, w_send.at[k, piece], k * 2 + core).wait_send()
+        for k, arrived, relay in arrivals:
+            if relay is not None and arrived == piece:
+                weight_copy(k * 2 + core, piece, w_relay.at[piece], relay * 2 + core).wait_send()
         for t in range(n_tile):
-            chip_copy(t, k).wait_send()
-    for k in range(n_chip):
-        weight_copy(k * 2 + core, w_sib.at[k], sibling).wait_send()
+            for k in direct + [diagonal] * square:
+                chip_copy(t, k, piece).wait_send()
+        for k in range(n_chip):
+            weight_copy(k * 2 + core, piece, w_sib.at[k, piece], sibling).wait_send()
     for t in range(n_tile):
         sib_copy(t).wait_send()
     for origin in range(n_mp):
@@ -335,7 +377,7 @@
     count, width = tokens.shape
     rows, units = weight_in.shape
     n_chip = n_dp // 2
-    n_ret = 8
+    n_ret = 4
     tile = min(256, units)
     n_tile = units // tile
     b16, f32 = jnp.bfloat16, jnp.float32
@@ -365,10 +407,10 @@
             pltpu.VMEM((n_tile, n_chip, 2, rows, tile), b16),
             pltpu.VMEM((n_tile, n_chip, 2, rows, tile), b16),
             dma((2, n_mp, 2)), dma((n_mp, 2)),
-            dma((n_chip,)), dma((n_chip,)), dma((n_dp,)),
+            dma((n_chip, 2)), dma((2,)), dma((n_chip, 2)), dma((n_dp, 2)),
             dma((n_mp, n_ret)), dma((n_mp + 1, n_ret)),
             dma((n_tile,)), dma((n_tile,)),
-            dma((n_tile, n_chip)), dma((n_tile, n_chip)),
+            dma((n_tile, n_chip, 2)), dma((n_tile, n_chip, 2)),
         ],
         compiler_params=pltpu.CompilerParams(
             collective_id=0, has_side_effects=True, vmem_limit_bytes=56 * 1024 * 1024

time: 127 us -> 122 us (0.961)
  Pallas kernels: 121 us -> 116 us
    pallas_call x1, Pallas kernels: 121 us -> 116 us  [shards(): pl.pallas_call(functools.partial(kernel, n_dp, n_mp, tile), out_shape=(ja...]
where the time goes in v5:
time: 122 us
  Pallas kernels  116 us (95%)
  other arithmetic  3.98 us (3%)
    pallas_call x1, Pallas kernels, shards(): pl.pallas_call(functools.partial(kernel, n_dp, n_mp, tile), out_shape=(ja...  116 us
    sub x2, other arithmetic, adam_step(): weight_new = weight - LEARN_RATE * (update + DECAY_RATE * weight)  3.98 us

profile of v5, /device:TPU:0, one launch (start us, length us, event | category | flops | bytes accessed | tf_op | source)
XLA Modules:
  0.0 121.9 jit_solution(9704768845200689383)
XLA Ops:
  0.6 0.0 copy-start
  0.6 0.0 copy-start.1
  0.7 0.0 copy-start.2
  0.7 116.3 %shard_map.135 = (bf16[256,1024]{1,0:T(8,128)(2,1)}, f32[128,1024]{1,0:T(8,128)}, f32[1024,128]{1,0:T(8,128)}) custom-call(bf16[256,1024]{1,0:T(8,128)(2,1)} %tokens_ref.1, bf16[256,1024]{1,0:T(8,128)(2,1)} %cot_ref.1, f32[128,1024]{1,0:T(8,128)} %win_ref.1, f32[1024,128]{1,0:T(8,128)} %wout_ref.1), custom_call_target="tpu_custom_call" | custom-call | flops 10737418240 | bytes 4194304 | tf_op jit(solution)/shard_map/pallas_call | solution.py:387
  117.0 0.0 copy-done
  117.0 0.0 copy-done.1
  117.0 0.0 copy-done.2
  117.0 0.0 copy-start.3
  117.0 0.0 copy-start.4
  117.0 0.0 copy-start.5
  117.1 0.0 copy-start.6
  117.1 2.6 %multiply_subtract_fusion.1 = (f32[128,1024]{1,0:T(8,128)}, f32[128,1024]{1,0:T(8,128)}, f32[128,1024]{1,0:T(8,128)}) fusion(f32[128,1024]{1,0:T(8,128)S(1)} %copy-done, f32[128,1024]{1,0:T(8,128)} %get-tuple-element.11, f32[128,1024]{1,0:T(8,128)S(1)} %copy-done.1, f32[128,1024]{1,0:T(8,128)S(1)} %copy-done.2), kind=kLoop, calls=%fused_computation.3 | loop fusion | flops 1966080 | bytes 3670016 | tf_op jit(solution)/shard_map/sub | solution.py:29
  119.7 0.0 copy-done.3
  119.7 0.0 copy-done.4
  119.7 0.0 copy-done.5
  119.7 0.0 copy-done.6
  119.7 0.0 copy-start.7
  119.7 1.4 %multiply_subtract_fusion = (f32[1024,128]{1,0:T(8,128)}, f32[1024,128]{1,0:T(8,128)}, f32[1024,128]{1,0:T(8,128)}) fusion(f32[1024,128]{1,0:T(8,128)S(1)} %copy-done.3, f32[1024,128]{1,0:T(8,128)S(1)} %copy-done.6, f32[1024,128]{1,0:T(8,128)S(1)} %copy-done.4, f32[1024,128]{1,0:T(8,128)S(1)} %copy-done.5), kind=kLoop, calls=%fused_computation | loop fusion | flops 1966080 | bytes 3670016 | tf_op jit(solution)/shard_map/sub | solution.py:29
  121.1 0.0 copy-done.7
  121.1 0.8 copy.16
Async XLA Ops:
  0.6 116.4 %copy-start = (f32[128,1024]{1,0:T(8,128)S(1)}, f32[128,1024]{1,0:T(8,128)}, u32[]{:S(2)}) copy-start(f32[128,1024]{1,0:T(8,128)} %win_ref.1) | copy-start | bytes 1572868
  0.6 116.4 %copy-start.1 = (f32[128,1024]{1,0:T(8,128)S(1)}, f32[128,1024]{1,0:T(8,128)}, u32[]{:S(2)}) copy-start(f32[128,1024]{1,0:T(8,128)} %param.13) | copy-start | bytes 1572868
  0.7 116.4 %copy-start.2 = (f32[128,1024]{1,0:T(8,128)S(1)}, f32[128,1024]{1,0:T(8,128)}, u32[]{:S(2)}) copy-start(f32[128,1024]{1,0:T(8,128)} %param.12) | copy-start | bytes 1572868
  117.0 2.7 %copy-start.3 = (f32[1024,128]{1,0:T(8,128)S(1)}, f32[1024,128]{1,0:T(8,128)}, u32[]{:S(2)}) copy-start(f32[1024,128]{1,0:T(8,128)} %wout_ref.1) | copy-start | bytes 1572868
  117.0 2.6 %copy-start.4 = (f32[1024,128]{1,0:T(8,128)S(1)}, f32[1024,128]{1,0:T(8,128)}, u32[]{:S(2)}) copy-start(f32[1024,128]{1,0:T(8,128)} %param.15) | copy-start | bytes 1572868
  117.0 2.6 %copy-start.5 = (f32[1024,128]{1,0:T(8,128)S(1)}, f32[1024,128]{1,0:T(8,128)}, u32[]{:S(2)}) copy-start(f32[1024,128]{1,0:T(8,128)} %param.14) | copy-start | bytes 1572868
  117.1 2.6 %copy-start.6 = (f32[1024,128]{1,0:T(8,128)S(1)}, f32[1024,128]{1,0:T(8,128)}, u32[]{:S(2)}) copy-start(f32[1024,128]{1,0:T(8,128)} %get-tuple-element.12) | copy-start | bytes 1572868
  119.7 1.4 %copy-start.7 = (bf16[256,1024]{1,0:T(8,128)(2,1)S(1)}, bf16[256,1024]{1,0:T(8,128)(2,1)}, u32[]{:S(2)}) copy-start(bf16[256,1024]{1,0:T(8,128)(2,1)} %get-tuple-element.26) | copy-start | bytes 1572868

commit v6 on v2

--- a/solution.py
+++ b/solution.py
@@ -42,7 +42,7 @@
     n_dp, n_mp, tile,
     tokens_ref, cot_ref, win_ref, wout_ref,
     ig_ref, gin_ref, gout_ref,
-    held, weights, grads, flipped, dn, own, ret_out, ret_in, sib_out, sib_in, chip_out, chip_in,
+    held, weights, grads, flipped, acts, dn, own, ret_out, ret_in, sib_out, sib_in, chip_out, chip_in,
     tok_send, tok_recv, w_send, w_sib, w_recv, ret_send, ret_recv, sib_send, sib_recv, chip_send, chip_recv,
 ):
     n_chip = n_dp // 2
@@ -188,9 +188,6 @@
     at_end = (z == 0) | (z == n_mp - 1)
 
     def chunk(origin, last):
-        flipped[0] = held[origin, 0].T
-        flipped[1] = held[origin, 1].T
-
         def columns(step, carry):
             part = pl.ds(pl.multiple_of(step * tile, tile), tile)
             w_in = weights[0, :, part]
@@ -198,8 +195,8 @@
             d_hidden = jnp.dot(held[origin, 1], weights[1, :, part], preferred_element_type=f32)
             hidden, slope = gelu_pair(preact)
             d_preact = (d_hidden * slope).astype(b16)
-            grads[0, :, part] += jnp.dot(flipped[0], d_preact, preferred_element_type=f32)
-            grads[1, :, part] += jnp.dot(flipped[1], hidden.astype(b16), preferred_element_type=f32)
+            acts[0, :, part] = d_preact
+            acts[1, :, part] = hidden.astype(b16)
             back = lax.dot_general(d_preact, w_in, (((1,), (1,)), ((), ())), preferred_element_type=f32)
 
             @pl.when(step == 0)
@@ -209,6 +206,30 @@
             @pl.when(step > 0)
             def _():
                 dn[...] += back
+            return carry
+
+        lax.fori_loop(0, n_tile, columns, 0)
+
+        @pl.when(origin == z)
+        def _():
+            own[...] = dn[...]
+
+        @pl.when(origin != z)
+        def _():
+            ret_out[origin] = dn[...].astype(b16)
+
+            @pl.when(at_end)
+            def _():
+                for step in range(n_ret):
+                    ret_copy(origin, step, jnp.where(z == 0, 1, -1)).start()
+
+        flipped[0] = held[origin, 0].T
+        flipped[1] = held[origin, 1].T
+
+        def gradients(step, carry):
+            part = pl.ds(pl.multiple_of(step * tile, tile), tile)
+            for piece in range(2):
+                grads[piece, :, part] += jnp.dot(flipped[piece], acts[piece, :, part], preferred_element_type=f32)
 
             @pl.when(last)
             def _():
@@ -219,20 +240,7 @@
                     chip_stage(step - 1)
             return carry
 
-        lax.fori_loop(0, n_tile, columns, 0)
-
-        @pl.when(origin == z)
-        def _():
-            own[...] = dn[...]
-
-        @pl.when(origin != z)
-        def _():
-            ret_out[origin] = dn[...].astype(b16)
-
-            @pl.when(at_end)
-            def _():
-                for step in range(n_ret):
-                    ret_copy(origin, step, jnp.where(z == 0, 1, -1)).start()
+        lax.fori_loop(0, n_tile, gradients, 0)
 
     def at_distance(distance, carry):
         @pl.when(distance >= 2)
@@ -255,14 +263,17 @@
     chip_stage(n_tile - 1)
 
     def hand_on(far, carry):
-        for step in range(n_ret):
+        for beat in range(n_ret + 1):
             for turn in range(2):
+                step = beat - turn
+                if not 0 <= step < n_ret:
+                    continue
                 down = (turn + z // (n_mp // 2)) % 2
                 way = 1 - 2 * down
                 target = far + down * (n_mp - 1 - 2 * far)
 
                 @pl.when(((target - z) * way > 0) & jnp.logical_not(at_end))
-                def _():
+                def _(step=step, way=way, target=target):
                     part = pl.ds(step * ret_rows, ret_rows)
                     ret_arrival(target, step).wait_recv()
                     ret_out[target, part] = (
@@ -350,6 +361,7 @@
             pltpu.VMEM((2, width, units), b16),
             pltpu.VMEM((2, width, units), f32),
             pltpu.VMEM((2, width, count), b16),
+            pltpu.VMEM((2, count, units), b16),
             pltpu.VMEM((count, width), f32),
             pltpu.VMEM((count, width), f32),
             pltpu.VMEM((n_mp, count, width), b16),

time: 119 us -> 116 us (0.975)
  Pallas kernels: 113 us -> 110 us
    pallas_call x1, Pallas kernels: 113 us -> 110 us  [shards(): pl.pallas_call(functools.partial(kernel, n_dp, n_mp, tile), out_shape=(ja...]
where the time goes in v6:
time: 116 us; the launch traced here: 115 us
  Pallas kernels  110 us (95%)
  other arithmetic  3.98 us (3%)
    pallas_call x1, Pallas kernels, shards(): pl.pallas_call(functools.partial(kernel, n_dp, n_mp, tile), out_shape=(ja...  110 us
    sub x2, other arithmetic, adam_step(): weight_new = weight - LEARN_RATE * (update + DECAY_RATE * weight)  3.98 us

profile of v6, /device:TPU:0, one launch (start us, length us, event | category | flops | bytes accessed | tf_op | source)
XLA Modules:
  0.0 115.5 jit_solution(9512489762550544534)
XLA Ops:
  0.6 0.0 copy-start
  0.6 0.0 copy-start.1
  0.7 0.0 copy-start.2
  0.7 109.9 %shard_map.135 = (bf16[256,1024]{1,0:T(8,128)(2,1)}, f32[128,1024]{1,0:T(8,128)}, f32[1024,128]{1,0:T(8,128)}) custom-call(bf16[256,1024]{1,0:T(8,128)(2,1)} %tokens_ref.1, bf16[256,1024]{1,0:T(8,128)(2,1)} %cot_ref.1, f32[128,1024]{1,0:T(8,128)} %win_ref.1, f32[1024,128]{1,0:T(8,128)} %wout_ref.1), custom_call_target="tpu_custom_call" | custom-call | flops 10737418240 | bytes 4194304 | tf_op jit(solution)/shard_map/pallas_call | solution.py:350
  110.6 0.0 copy-done
  110.6 0.0 copy-done.1
  110.6 0.0 copy-done.2
  110.6 0.0 copy-start.3
  110.6 0.0 copy-start.4
  110.6 0.0 copy-start.5
  110.6 0.0 copy-start.6
  110.7 2.6 %multiply_subtract_fusion.1 = (f32[128,1024]{1,0:T(8,128)}, f32[128,1024]{1,0:T(8,128)}, f32[128,1024]{1,0:T(8,128)}) fusion(f32[128,1024]{1,0:T(8,128)S(1)} %copy-done, f32[128,1024]{1,0:T(8,128)} %get-tuple-element.11, f32[128,1024]{1,0:T(8,128)S(1)} %copy-done.1, f32[128,1024]{1,0:T(8,128)S(1)} %copy-done.2), kind=kLoop, calls=%fused_computation.3 | loop fusion | flops 1966080 | bytes 3670016 | tf_op jit(solution)/shard_map/sub | solution.py:29
  113.3 0.0 copy-done.3
  113.3 0.0 copy-done.4
  113.3 0.0 copy-done.5
  113.3 0.0 copy-done.6
  113.3 0.0 copy-start.7
  113.3 1.4 %multiply_subtract_fusion = (f32[1024,128]{1,0:T(8,128)}, f32[1024,128]{1,0:T(8,128)}, f32[1024,128]{1,0:T(8,128)}) fusion(f32[1024,128]{1,0:T(8,128)S(1)} %copy-done.3, f32[1024,128]{1,0:T(8,128)S(1)} %copy-done.6, f32[1024,128]{1,0:T(8,128)S(1)} %copy-done.4, f32[1024,128]{1,0:T(8,128)S(1)} %copy-done.5), kind=kLoop, calls=%fused_computation | loop fusion | flops 1966080 | bytes 3670016 | tf_op jit(solution)/shard_map/sub | solution.py:29
  114.7 0.0 copy-done.7
  114.7 0.8 copy.16
Async XLA Ops:
  0.6 110.0 %copy-start = (f32[128,1024]{1,0:T(8,128)S(1)}, f32[128,1024]{1,0:T(8,128)}, u32[]{:S(2)}) copy-start(f32[128,1024]{1,0:T(8,128)} %win_ref.1) | copy-start | bytes 1572868
  0.6 110.0 %copy-start.1 = (f32[128,1024]{1,0:T(8,128)S(1)}, f32[128,1024]{1,0:T(8,128)}, u32[]{:S(2)}) copy-start(f32[128,1024]{1,0:T(8,128)} %param.13) | copy-start | bytes 1572868
  0.7 110.0 %copy-start.2 = (f32[128,1024]{1,0:T(8,128)S(1)}, f32[128,1024]{1,0:T(8,128)}, u32[]{:S(2)}) copy-start(f32[128,1024]{1,0:T(8,128)} %param.12) | copy-start | bytes 1572868
  110.6 2.7 %copy-start.3 = (f32[1024,128]{1,0:T(8,128)S(1)}, f32[1024,128]{1,0:T(8,128)}, u32[]{:S(2)}) copy-start(f32[1024,128]{1,0:T(8,128)} %wout_ref.1) | copy-start | bytes 1572868
  110.6 2.6 %copy-start.4 = (f32[1024,128]{1,0:T(8,128)S(1)}, f32[1024,128]{1,0:T(8,128)}, u32[]{:S(2)}) copy-start(f32[1024,128]{1,0:T(8,128)} %param.15) | copy-start | bytes 1572868
  110.6 2.6 %copy-start.5 = (f32[1024,128]{1,0:T(8,128)S(1)}, f32[1024,128]{1,0:T(8,128)}, u32[]{:S(2)}) copy-start(f32[1024,128]{1,0:T(8,128)} %param.14) | copy-start | bytes 1572868
  110.6 2.6 %copy-start.6 = (f32[1024,128]{1,0:T(8,128)S(1)}, f32[1024,128]{1,0:T(8,128)}, u32[]{:S(2)}) copy-start(f32[1024,128]{1,0:T(8,128)} %get-tuple-element.12) | copy-start | bytes 1572868
  113.3 1.4 %copy-start.7 = (bf16[256,1024]{1,0:T(8,128)(2,1)S(1)}, bf16[256,1024]{1,0:T(8,128)(2,1)}, u32[]{:S(2)}) copy-start(bf16[256,1024]{1,0:T(8,128)(2,1)} %get-tuple-element.26) | copy-start | bytes 1572868

commit v7 on v5

--- a/solution.py
+++ b/solution.py
@@ -42,7 +42,7 @@
     n_dp, n_mp, tile,
     tokens_ref, cot_ref, win_ref, wout_ref,
     ig_ref, gin_ref, gout_ref,
-    held, weights, grads, flipped, dn, own, ret_out, ret_in, sib_out, sib_in, chip_out, chip_in,
+    held, weights, grads, flipped, acts, dn, own, ret_out, ret_in, sib_out, sib_in, chip_out, chip_in,
     tok_send, tok_recv, w_send, w_relay, w_sib, w_recv, ret_send, ret_recv, sib_send, sib_recv, chip_send, chip_recv,
 ):
     n_chip = n_dp // 2
@@ -66,6 +66,15 @@
     for i in range(1, n_mp):
         pl.semaphore_signal(barrier, inc=1, device_id=(dp, (z + i) % n_mp), device_id_type=MESH)
 
+    values = tokens_ref[...].astype(f32)
+    inverse = lax.rsqrt(jnp.mean(values * values, axis=-1, keepdims=True) + 1e-06)
+    held[z, 0] = (values * inverse).astype(b16)
+    held[z, 1] = cot_ref[...]
+    own_rows = pl.ds(pl.multiple_of(dp * rows, rows), rows)
+    weights[0, own_rows, :] = win_ref[...].astype(b16)
+    weights[1, own_rows, :] = wout_ref[...].T.astype(b16)
+    pl.semaphore_wait(barrier, n_chip + n_mp - 1)
+
     def tok_copy(origin, piece, side, target):
         return pltpu.make_async_remote_copy(
             src_ref=held.at[origin, piece], dst_ref=held.at[origin, piece],
@@ -157,29 +166,20 @@
                 ).astype(b16)
                 chip_copy(t, k, piece).start()
 
-    def send_own(piece):
-        @pl.when(z < n_mp - 1)
-        def _():
+    @pl.when(z < n_mp - 1)
+    def _():
+        for piece in range(2):
             tok_copy(z, piece, 0, z + 1).start()
 
-        @pl.when(z > 0)
-        def _():
+    @pl.when(z > 0)
+    def _():
+        for piece in range(2):
             tok_copy(z, piece, 1, z - 1).start()
 
-    held[z, 1] = cot_ref[...]
-    own_rows = pl.ds(pl.multiple_of(dp * rows, rows), rows)
-    weights[0, own_rows, :] = win_ref[...].astype(b16)
-    weights[1, own_rows, :] = wout_ref[...].T.astype(b16)
-    pl.semaphore_wait(barrier, n_chip + n_mp - 1)
-    send_own(1)
     for piece in range(2):
         for k in direct:
             weight_copy(dp, piece, w_send.at[k, piece], k * 2 + core).start()
         weight_copy(dp, piece, w_sib.at[chip, piece], sibling).start()
-    values = tokens_ref[...].astype(f32)
-    inverse = lax.rsqrt(jnp.mean(values * values, axis=-1, keepdims=True) + 1e-06)
-    held[z, 0] = (values * inverse).astype(b16)
-    send_own(0)
 
     def clear(i, carry):
         part = pl.ds(pl.multiple_of(i * rows, rows), rows)
@@ -195,7 +195,7 @@
         weight_copy(k * 2 + core, piece, w_sib.at[k, piece], sibling).start()
 
     def pass_on(distance):
-        for piece in (1, 0):
+        for piece in range(2):
             @pl.when(z - distance >= 0)
             def _():
                 tok_copy(z - distance, piece, 0, z).wait_recv()
@@ -212,19 +212,15 @@
                 def _():
                     tok_copy(z + distance, piece, 1, z - 1).start()
 
-    at_end = (z == 0) | (z == n_mp - 1)
-
     pass_on(1)
     for k in range(n_chip):
         for piece in range(2):
             weight_copy(k * 2 + (1 - core), piece, w_sib.at[k, piece], sibling).wait_recv()
 
     furthest = jnp.where(z > n_mp - 1 - z, z, n_mp - 1 - z)
+    at_end = (z == 0) | (z == n_mp - 1)
 
     def chunk(origin, last):
-        flipped[0] = held[origin, 0].T
-        flipped[1] = held[origin, 1].T
-
         def columns(step, carry):
             part = pl.ds(pl.multiple_of(step * tile, tile), tile)
             w_in = weights[0, :, part]
@@ -232,8 +228,8 @@
             d_hidden = jnp.dot(held[origin, 1], weights[1, :, part], preferred_element_type=f32)
             hidden, slope = gelu_pair(preact)
             d_preact = (d_hidden * slope).astype(b16)
-            grads[0, :, part] += jnp.dot(flipped[0], d_preact, preferred_element_type=f32)
-            grads[1, :, part] += jnp.dot(flipped[1], hidden.astype(b16), preferred_element_type=f32)
+            acts[0, :, part] = d_preact
+            acts[1, :, part] = hidden.astype(b16)
             back = lax.dot_general(d_preact, w_in, (((1,), (1,)), ((), ())), preferred_element_type=f32)
 
             @pl.when(step == 0)
@@ -243,6 +239,30 @@
             @pl.when(step > 0)
             def _():
                 dn[...] += back
+            return carry
+
+        lax.fori_loop(0, n_tile, columns, 0)
+
+        @pl.when(origin == z)
+        def _():
+            own[...] = dn[...]
+
+        @pl.when(origin != z)
+        def _():
+            ret_out[origin] = dn[...].astype(b16)
+
+            @pl.when(at_end)
+            def _():
+                for step in range(n_ret):
+                    ret_copy(origin, step, jnp.where(z == 0, 1, -1)).start()
+
+        flipped[0] = held[origin, 0].T
+        flipped[1] = held[origin, 1].T
+
+        def gradients(step, carry):
+            part = pl.ds(pl.multiple_of(step * tile, tile), tile)
+            for piece in range(2):
+                grads[piece, :, part] += jnp.dot(flipped[piece], acts[piece, :, part], preferred_element_type=f32)
 
             @pl.when(last)
             def _():
@@ -251,35 +271,16 @@
                 @pl.when(step > 0)
                 def _():
                     chip_stage(step - 1)
-
-                @pl.when(step > 1)
-                def _():
-                    relay_stage(step - 2)
             return carry
 
-        lax.fori_loop(0, n_tile, columns, 0)
-
-        @pl.when(origin == z)
+        lax.fori_loop(0, n_tile, gradients, 0)
+
+    def at_distance(distance, carry):
+        @pl.when(distance >= 2)
         def _():
-            own[...] = dn[...]
-
-        @pl.when(origin != z)
-        def _():
-            ret_out[origin] = dn[...].astype(b16)
-
-            @pl.when(at_end)
-            def _():
-                for step in range(n_ret):
-                    ret_copy(origin, step, jnp.where(z == 0, 1, -1)).start()
-
-    def at_distance(distance, carry):
+            pass_on(distance)
+
         def side(which, inner):
-            ahead = distance + which
-
-            @pl.when((ahead >= 2) & (ahead < n_mp) & (which == jnp.where(at_end, 0, 1)))
-            def _():
-                pass_on(ahead)
-
             origin = z + distance * (2 * which - 1)
 
             @pl.when((origin >= 0) & (origin < n_mp) & (distance + which > 0))
@@ -293,18 +294,21 @@
     lax.fori_loop(0, n_mp, at_distance, 0)
 
     chip_stage(n_tile - 1)
-    for t in range(max(0, n_tile - 2), n_tile):
+    for t in range(n_tile):
         relay_stage(t)
 
     def hand_on(far, carry):
-        for step in range(n_ret):
+        for beat in range(n_ret + 1):
             for turn in range(2):
+                step = beat - turn
+                if not 0 <= step < n_ret:
+                    continue
                 down = (turn + z // (n_mp // 2)) % 2
                 way = 1 - 2 * down
                 target = far + down * (n_mp - 1 - 2 * far)
 
                 @pl.when(((target - z) * way > 0) & jnp.logical_not(at_end))
-                def _():
+                def _(step=step, way=way, target=target):
                     part = pl.ds(step * ret_rows, ret_rows)
                     ret_arrival(target, step).wait_recv()
                     ret_out[target, part] = (
@@ -398,6 +402,7 @@
             pltpu.VMEM((2, width, units), b16),
             pltpu.VMEM((2, width, units), f32),
             pltpu.VMEM((2, width, count), b16),
+            pltpu.VMEM((2, count, units), b16),
             pltpu.VMEM((count, width), f32),
             pltpu.VMEM((count, width), f32),
             pltpu.VMEM((n_mp, count, width), b16),

time: 122 us -> 108 us (0.89)
  Pallas kernels: 116 us -> 103 us
    pallas_call x1, Pallas kernels: 116 us -> 103 us  [shards(): pl.pallas_call(functools.partial(kernel, n_dp, n_mp, tile), out_shape=(ja...]
where the time goes in v7:
time: 108 us
  Pallas kernels  103 us (95%)
  other arithmetic  3.98 us (4%)
    pallas_call x1, Pallas kernels, shards(): pl.pallas_call(functools.partial(kernel, n_dp, n_mp, tile), out_shape=(ja...  103 us
    sub x2, other arithmetic, adam_step(): weight_new = weight - LEARN_RATE * (update + DECAY_RATE * weight)  3.98 us

profile of v7, /device:TPU:0, one launch (start us, length us, event | category | flops | bytes accessed | tf_op | source)
XLA Modules:
  0.0 108.2 jit_solution(6549771142873086916)
XLA Ops:
  0.6 0.0 copy-start
  0.6 0.0 copy-start.1
  0.7 0.0 copy-start.2
  0.7 102.7 %shard_map.135 = (bf16[256,1024]{1,0:T(8,128)(2,1)}, f32[128,1024]{1,0:T(8,128)}, f32[1024,128]{1,0:T(8,128)}) custom-call(bf16[256,1024]{1,0:T(8,128)(2,1)} %tokens_ref.1, bf16[256,1024]{1,0:T(8,128)(2,1)} %cot_ref.1, f32[128,1024]{1,0:T(8,128)} %win_ref.1, f32[1024,128]{1,0:T(8,128)} %wout_ref.1), custom_call_target="tpu_custom_call" | custom-call | flops 10737418240 | bytes 4194304 | tf_op jit(solution)/shard_map/pallas_call | solution.py:391
  103.4 0.0 copy-done
  103.4 0.0 copy-done.1
  103.4 0.0 copy-done.2
  103.4 0.0 copy-start.3
  103.4 0.0 copy-start.4
  103.4 0.0 copy-start.5
  103.4 0.0 copy-start.6
  103.4 2.6 %multiply_subtract_fusion.1 = (f32[128,1024]{1,0:T(8,128)}, f32[128,1024]{1,0:T(8,128)}, f32[128,1024]{1,0:T(8,128)}) fusion(f32[128,1024]{1,0:T(8,128)S(1)} %copy-done, f32[128,1024]{1,0:T(8,128)} %get-tuple-element.11, f32[128,1024]{1,0:T(8,128)S(1)} %copy-done.1, f32[128,1024]{1,0:T(8,128)S(1)} %copy-done.2), kind=kLoop, calls=%fused_computation.3 | loop fusion | flops 1966080 | bytes 3670016 | tf_op jit(solution)/shard_map/sub | solution.py:29
  106.0 0.0 copy-done.3
  106.0 0.0 copy-done.4
  106.0 0.0 copy-done.5
  106.0 0.0 copy-done.6
  106.1 0.0 copy-start.7
  106.1 1.4 %multiply_subtract_fusion = (f32[1024,128]{1,0:T(8,128)}, f32[1024,128]{1,0:T(8,128)}, f32[1024,128]{1,0:T(8,128)}) fusion(f32[1024,128]{1,0:T(8,128)S(1)} %copy-done.3, f32[1024,128]{1,0:T(8,128)S(1)} %copy-done.6, f32[1024,128]{1,0:T(8,128)S(1)} %copy-done.4, f32[1024,128]{1,0:T(8,128)S(1)} %copy-done.5), kind=kLoop, calls=%fused_computation | loop fusion | flops 1966080 | bytes 3670016 | tf_op jit(solution)/shard_map/sub | solution.py:29
  107.4 0.0 copy-done.7
  107.4 0.8 copy.16
Async XLA Ops:
  0.6 102.7 %copy-start = (f32[128,1024]{1,0:T(8,128)S(1)}, f32[128,1024]{1,0:T(8,128)}, u32[]{:S(2)}) copy-start(f32[128,1024]{1,0:T(8,128)} %win_ref.1) | copy-start | bytes 1572868
  0.6 102.7 %copy-start.1 = (f32[128,1024]{1,0:T(8,128)S(1)}, f32[128,1024]{1,0:T(8,128)}, u32[]{:S(2)}) copy-start(f32[128,1024]{1,0:T(8,128)} %param.13) | copy-start | bytes 1572868
  0.7 102.7 %copy-start.2 = (f32[128,1024]{1,0:T(8,128)S(1)}, f32[128,1024]{1,0:T(8,128)}, u32[]{:S(2)}) copy-start(f32[128,1024]{1,0:T(8,128)} %param.12) | copy-start | bytes 1572868
  103.4 2.7 %copy-start.3 = (f32[1024,128]{1,0:T(8,128)S(1)}, f32[1024,128]{1,0:T(8,128)}, u32[]{:S(2)}) copy-start(f32[1024,128]{1,0:T(8,128)} %wout_ref.1) | copy-start | bytes 1572868
  103.4 2.6 %copy-start.4 = (f32[1024,128]{1,0:T(8,128)S(1)}, f32[1024,128]{1,0:T(8,128)}, u32[]{:S(2)}) copy-start(f32[1024,128]{1,0:T(8,128)} %param.15) | copy-start | bytes 1572868
  103.4 2.6 %copy-start.5 = (f32[1024,128]{1,0:T(8,128)S(1)}, f32[1024,128]{1,0:T(8,128)}, u32[]{:S(2)}) copy-start(f32[1024,128]{1,0:T(8,128)} %param.14) | copy-start | bytes 1572868
  103.4 2.6 %copy-start.6 = (f32[1024,128]{1,0:T(8,128)S(1)}, f32[1024,128]{1,0:T(8,128)}, u32[]{:S(2)}) copy-start(f32[1024,128]{1,0:T(8,128)} %get-tuple-element.12) | copy-start | bytes 1572868
  106.1 1.4 %copy-start.7 = (bf16[256,1024]{1,0:T(8,128)(2,1)S(1)}, bf16[256,1024]{1,0:T(8,128)(2,1)}, u32[]{:S(2)}) copy-start(bf16[256,1024]{1,0:T(8,128)(2,1)} %get-tuple-element.26) | copy-start | bytes 1572868
